TPU v7x, 512 devices: a whole 4x4x16 slice. The times are simulated.
512 devices in a mesh: ctx: 128 (over x, z, core), head: 4 (over y).
Axes of the slice: x: 4, y: 4, z: 16, core: 2. Of those that a mesh axis runs over, the one named last changes fastest.
Arguments:
- query: bfloat16 [32768, 20, 128], P('ctx', 'head'), may hold values from -12 to 12
- key: bfloat16 [32768, 20, 128], P('ctx', 'head'), may hold values from -12 to 12
- value: bfloat16 [32768, 20, 128], P('ctx', 'head'), may hold values from -6 to 6
- query_gain: float32 [20, 128], P('head'), may hold values from 0.1 to 1.9
- key_gain: float32 [20, 128], P('head'), may hold values from 0.1 to 1.9
- head_class: int32 [20], P('head'), may hold values from 0 to 1, as said below
- neighbours: int32 [128, 7], P('ctx'), may hold values from 0 to 127, as said below
- tiles: int32 [128, 7, 4, 4], P('ctx'), may hold values from 0 to 1, as said below
Outputs:
- attended: bfloat16 [32768, 20, 128], P('ctx', 'head')
Inputs may be any that keep to these rules, and one draw needn't show every extreme that they name: `head_class`: each aligned group of 5 heads holds exactly 2 temporal heads. `neighbours`: entry 0 of frame f is f; every entry lies within 3 frames of f. For block 0, tiles with equal query and key tile are 1.
All inputs are finite; a program needn't handle non-finite values.
Results may differ from a plain program's by a relative error of at most 0.0081.
Values may be sent and summed in bfloat16 or wider, within the bound.
No kernel may reach another device: no remote copies, remote signals or barrier semaphores. Data moves between devices by JAX's collectives and lax.ppermute only.
A program may use at most 64 MiB of HBM per device.

v0:
```python
import jax
import jax.numpy as jnp
from jax import lax
from jax.sharding import PartitionSpec as P

HEAD_SIZE = 128
TEMP = 2
FRAME_POS = 256
NB = 7
TILE = 64
REACH = 3


def shifted(block, axis, distance):
    devices = range(lax.axis_size(axis))
    route = [(i - distance, i) for i in devices if i - distance in devices]
    return lax.ppermute(block, axis, route)


def softened(scores):
    top = jnp.max(scores, axis=-1, keepdims=True)
    expo = jnp.exp(scores - top)
    return (expo / jnp.sum(expo, axis=-1, keepdims=True)).astype(jnp.bfloat16)


def shards(query, key, value, query_gain, key_gain, head_class, neighbours, tiles):
    tok_count, group, size = query.shape
    frames_dev = neighbours.shape[0]
    scale = HEAD_SIZE ** (-0.5)
    query_f = query.astype(jnp.float32)
    key_f = key.astype(jnp.float32)
    sums_query, sums_key = lax.psum(
        (jnp.sum(query_f * query_f, axis=(1, 2)), jnp.sum(key_f * key_f, axis=(1, 2))), "head"
    )
    entries = group * lax.axis_size("head") * size
    normed_query = (
        query_f * lax.rsqrt(sums_query / entries + 1e-06)[:, None, None] * query_gain[None]
    ).astype(jnp.bfloat16)
    normed_key = (
        key_f * lax.rsqrt(sums_key / entries + 1e-06)[:, None, None] * key_gain[None]
    ).astype(jnp.bfloat16)
    order = jnp.argsort(head_class, stable=True)
    n_spatial = group - TEMP
    spatial_heads = order[:n_spatial]
    temporal_heads = order[n_spatial:]
    paired = jnp.stack(
        (jnp.take(normed_key, spatial_heads, axis=1), jnp.take(value, spatial_heads, axis=1))
    )
    hops = REACH // frames_dev
    pieces = []
    for offset in range(-hops, hops + 1):
        if offset == 0:
            pieces.append(paired)
        else:
            pieces.append(shifted(paired, "ctx", -offset))
    window = jnp.concatenate(pieces, axis=1)
    window = window.reshape(2, (2 * hops + 1) * frames_dev, FRAME_POS, n_spatial, size)
    first_frame = (lax.axis_index("ctx") - hops) * frames_dev
    local_frames = (neighbours - first_frame).reshape(-1)
    picked = jnp.take(window, local_frames, axis=1).reshape(
        2, frames_dev, NB * FRAME_POS, n_spatial, size
    )
    spatial_query = jnp.take(normed_query, spatial_heads, axis=1).reshape(
        frames_dev, FRAME_POS, n_spatial, size
    )
    grown = jnp.repeat(jnp.repeat(tiles, TILE, axis=2), TILE, axis=3)
    allowed = jnp.transpose(grown, (0, 2, 1, 3)).reshape(frames_dev, FRAME_POS, NB * FRAME_POS) > 0

    def head_block(items):
        q_head, k_head, v_head = items
        head_scores = (
            jnp.einsum("fqd,fkd->fqk", q_head, k_head, preferred_element_type=jnp.float32) * scale
        )
        head_scores = jnp.where(allowed, head_scores, -jnp.inf)
        head_weights = softened(head_scores)
        return jnp.einsum(
            "fqk,fkd->fqd", head_weights, v_head, preferred_element_type=jnp.float32
        ).astype(jnp.bfloat16)

    per_head = lax.map(
        head_block,
        (
            jnp.moveaxis(spatial_query, 2, 0),
            jnp.moveaxis(picked[0], 2, 0),
            jnp.moveaxis(picked[1], 2, 0),
        ),
    )
    spatial_out = jnp.moveaxis(per_head, 0, 2).reshape(tok_count, n_spatial, size)
    shape4 = (frames_dev, FRAME_POS, TEMP, size)
    temp_query = jnp.take(normed_query, temporal_heads, axis=1).reshape(shape4)
    temp_key = jnp.take(normed_key, temporal_heads, axis=1).reshape(shape4)
    temp_value = jnp.take(value, temporal_heads, axis=1).reshape(shape4)
    rows_q = lax.all_to_all(temp_query, "ctx", split_axis=1, concat_axis=0, tiled=True)
    rows_k = lax.all_to_all(temp_key, "ctx", split_axis=1, concat_axis=0, tiled=True)
    rows_v = lax.all_to_all(temp_value, "ctx", split_axis=1, concat_axis=0, tiled=True)
    temporal_scores = (
        jnp.einsum("fphd,gphd->phfg", rows_q, rows_k, preferred_element_type=jnp.float32) * scale
    )
    temporal_weights = softened(temporal_scores)
    outputs = jnp.einsum(
        "phfg,gphd->fphd", temporal_weights, rows_v, preferred_element_type=jnp.float32
    ).astype(jnp.bfloat16)
    temporal_out = lax.all_to_all(outputs, "ctx", split_axis=0, concat_axis=1, tiled=True)
    temporal_out = temporal_out.reshape(tok_count, TEMP, size)
    joined = jnp.concatenate([spatial_out, temporal_out], axis=1)
    inverse = jnp.argsort(order)
    return jnp.take(joined, inverse, axis=1)


def solution(mesh):
    in_specs = (
        P("ctx", "head", None),
        P("ctx", "head", None),
        P("ctx", "head", None),
        P("head", None),
        P("head", None),
        P("head"),
        P("ctx", None),
        P("ctx", None, None, None),
    )
    out_specs = P("ctx", "head", None)
    return jax.shard_map(shards, mesh=mesh, in_specs=in_specs, out_specs=out_specs, check_vma=False)
```

profile of v0, /device:TPU:1, one launch (start us, length us, event | category | flops | bytes accessed | tf_op | source)
XLA Modules:
  0.0 159.7 jit_solution(10054433793856028611)
XLA Ops:
  2.3 1.6 %sort.34 = (s32[5]{0:T(128)}, s32[5]{0:T(128)S(1)}) sort(s32[5]{0:T(128)} %param.19, s32[5]{0:T(128)S(1)} %iota.8), dimensions={0}, to_apply=%region_0.0 | sort | flops 15 | bytes 80 | tf_op jit(solution)/shard_map/jit(argsort)/sort | solution.py:42
  3.9 9.5 %all-reduce = (f32[256]{0:T(256)S(1)}, f32[256]{0:T(256)S(1)}) all-reduce(f32[256]{0:T(256)S(1)} %fusion.21, f32[256]{0:T(256)S(1)} %fusion.18), channel_id=1, replica_groups=mesh['ctx'=128,'head'=4] {'head'}, use_global_device_ids=true, to_apply=%region_5.7 | all-reduce | flops 512 | bytes 4096 | tf_op jit(solution)/shard_map/psum | solution.py:32
  19.8 7.5 %collective-permute-start = (bf16[2,256,3,128]{3,1,2,0:T(8,128)(2,1)}, bf16[2,256,3,128]{3,1,2,0:T(8,128)(2,1)S(1)}, u32[]{:S(2)}, u32[]{:S(2)}) collective-permute-start(bf16[2,256,3,128]{3,1,2,0:T(8,128)(2,1)} %pad_maximum_fusion), channel_id=1, source_target_pairs={{0,12},{4,16},{8,20},{12,24},{16,28},{20,32},{24,36},{28,40},{32,4... | collective-permute-start | bytes 1179656 | tf_op jit(solution)/shard_map/ppermute | solution.py:17
  27.3 4.3 %collective-permute-start.1 = (bf16[2,256,3,128]{3,1,2,0:T(8,128)(2,1)}, bf16[2,256,3,128]{3,1,2,0:T(8,128)(2,1)}, u32[]{:S(2)}, u32[]{:S(2)}) collective-permute-start(bf16[2,256,3,128]{3,1,2,0:T(8,128)(2,1)} %pad_maximum_fusion), channel_id=1, source_target_pairs={{0,8},{4,12},{8,16},{12,20},{16,24},{20,28},{24,32},{28,36},{32,40... | collective-permute-start | bytes 1179656 | tf_op jit(solution)/shard_map/ppermute | solution.py:17
  31.6 1.9 %collective-permute-start.2 = (bf16[2,256,3,128]{3,1,2,0:T(8,128)(2,1)}, bf16[2,256,3,128]{3,1,2,0:T(8,128)(2,1)}, u32[]{:S(2)}, u32[]{:S(2)}) collective-permute-start(bf16[2,256,3,128]{3,1,2,0:T(8,128)(2,1)} %pad_maximum_fusion), channel_id=1, source_target_pairs={{0,4},{4,8},{8,12},{12,16},{16,20},{20,24},{24,28},{28,32},{32,36}... | collective-permute-start | bytes 1179656 | tf_op jit(solution)/shard_map/ppermute | solution.py:17
  33.5 3.2 %collective-permute-start.3 = (bf16[2,256,3,128]{3,1,2,0:T(8,128)(2,1)}, bf16[2,256,3,128]{3,1,2,0:T(8,128)(2,1)}, u32[]{:S(2)}, u32[]{:S(2)}) collective-permute-start(bf16[2,256,3,128]{3,1,2,0:T(8,128)(2,1)} %pad_maximum_fusion), channel_id=1, source_target_pairs={{4,0},{8,4},{12,8},{16,12},{20,16},{24,20},{28,24},{32,28},{36,32}... | collective-permute-start | bytes 1179656 | tf_op jit(solution)/shard_map/ppermute | solution.py:17
  36.7 1.3 collective-permute-start.4
  41.6 18.6 %all-to-all-start.2 = ((bf16[1,256,2,128]{3,2,0,1:T(2,128)(2,1)}), bf16[1,256,2,128]{3,2,0,1:T(2,128)(2,1)}, u32[]{:S(2)}, u32[]{:S(2)}) async-start(bf16[1,256,2,128]{3,2,0,1:T(2,128)(2,1)} %copy.58), calls=%async_computation.2 | async-start | bytes 262144 | tf_op jit(solution)/shard_map/all_to_all | solution.py:94
  68.6 8.7 %all-to-all-done.2 = bf16[1,256,2,128]{3,2,0,1:T(2,128)(2,1)} async-done(((bf16[1,256,2,128]{3,2,0,1:T(2,128)(2,1)}), bf16[1,256,2,128]{3,2,0,1:T(2,128)(2,1)}, u32[]{:S(2)}, u32[]{:S(2)}) %all-to-all-start.2) | async-done | bytes 131104 | tf_op jit(solution)/shard_map/all_to_all | solution.py:94
  77.2 8.9 %all-to-all-start.1 = ((bf16[1,256,2,128]{3,2,0,1:T(2,128)(2,1)}), bf16[1,256,2,128]{3,2,0,1:T(2,128)(2,1)}, u32[]{:S(2)}, u32[]{:S(2)}) async-start(bf16[1,256,2,128]{3,2,0,1:T(2,128)(2,1)} %copy.56), calls=%async_computation.1 | async-start | bytes 262144 | tf_op jit(solution)/shard_map/all_to_all | solution.py:93
  88.3 1.5 copy-done.1
  89.9 2.0 %copy.47 = bf16[2,7,256,3,128]{4,2,3,1,0:T(8,128)(2,1)S(1)} copy(bf16[2,7,256,3,128]{4,2,1,3,0:T(8,128)(2,1)} %bitcast.99) | data formatting | bytes 5505024 | tf_op jit(solution)/shard_map/reshape | solution.py:57
  91.8 2.5 %gather_fusion = bf16[7,2,256,3,128]{4,2,3,1,0:T(8,128)(2,1)} fusion(bf16[2,7,256,3,128]{4,2,3,1,0:T(8,128)(2,1)S(1)} %copy.47, s32[1024]{0:T(1024)S(1)} %get-tuple-element.109), kind=kCustom, calls=%fused_computation.6 | custom fusion | bytes 5505052 | tf_op jit(solution)/shard_map/jit(_take)/gather | solution.py:60
  94.3 2.1 %select_bitcast_fusion = bf16[2,7,256,3,128]{4,2,3,0,1:T(8,128)(2,1)S(1)} fusion(bf16[7,2,256,3,128]{4,2,3,1,0:T(8,128)(2,1)} %gather_fusion, pred[7]{0:T(512)(128)(4,1)S(1)} %compare_and_fusion.2), kind=kLoop, calls=%fused_computation.26 | loop fusion | flops 1376256 | bytes 5505031 | tf_op jit(solution)/shard_map/jit(_take)/select_n | solution.py:60
  96.4 6.8 %all-to-all-done.1 = bf16[1,256,2,128]{3,2,0,1:T(2,128)(2,1)} async-done(((bf16[1,256,2,128]{3,2,0,1:T(2,128)(2,1)}), bf16[1,256,2,128]{3,2,0,1:T(2,128)(2,1)}, u32[]{:S(2)}, u32[]{:S(2)}) %all-to-all-start.1) | async-done | bytes 131104 | tf_op jit(solution)/shard_map/all_to_all | solution.py:93
  103.2 9.4 %all-to-all-start = ((bf16[1,256,2,128]{3,2,0,1:T(2,128)(2,1)}), bf16[1,256,2,128]{3,2,0,1:T(2,128)(2,1)S(1)}, u32[]{:S(2)}, u32[]{:S(2)}) async-start(bf16[1,256,2,128]{3,2,0,1:T(2,128)(2,1)} %copy.54), calls=%async_computation | async-start | bytes 262144 | tf_op jit(solution)/shard_map/all_to_all | solution.py:95
  115.6 14.3 %all-to-all-done = bf16[1,256,2,128]{3,2,0,1:T(2,128)(2,1)S(1)} async-done(((bf16[1,256,2,128]{3,2,0,1:T(2,128)(2,1)}), bf16[1,256,2,128]{3,2,0,1:T(2,128)(2,1)S(1)}, u32[]{:S(2)}, u32[]{:S(2)}) %all-to-all-start) | async-done | bytes 131104 | tf_op jit(solution)/shard_map/all_to_all | solution.py:95
  130.8 1.7 %copy.64 = bf16[128,2,2,128]{3,2,1,0:T(2,128)(2,1)} copy(bf16[128,2,2,128]{0,3,2,1:T(8,128)(2,1)} %fusion.17) | data formatting | bytes 262144 | tf_op jit(solution)/shard_map/convert_element_type | solution.py:102
  132.4 7.2 %all-to-all-start.3 = ((bf16[128,2,2,128]{3,2,1,0:T(2,128)(2,1)}), bf16[128,2,2,128]{3,2,1,0:T(2,128)(2,1)S(1)}, u32[]{:S(2)}, u32[]{:S(2)}) async-start(bf16[128,2,2,128]{3,2,1,0:T(2,128)(2,1)} %copy.64), calls=%async_computation.3 | async-start | bytes 262144 | tf_op jit(solution)/shard_map/all_to_all | solution.py:103
  139.7 10.9 %while.11 = (s32[]{:T(128)}, bf16[3,1,256,128]{3,2,1,0:T(8,128)(2,1)}, bf16[3,1,256,128]{3,2,1,0:T(8,128)(2,1)}, bf16[3,1,1792,128]{3,2,1,0:T(8,128)(2,1)S(1)}, ...) while((s32[]{:T(128)}, ...), condition=%wide.region_9.11_spmd.clone, body=%wide.region_6.10_spmd.clone.sunk | while | flops 238583296 | bytes 8403029 | solution.py:80
  140.4 1.4 fusion.48
  144.0 1.4 fusion.48
  147.6 1.4 fusion.48
  150.5 6.7 %all-to-all-done.3 = bf16[128,2,2,128]{3,2,1,0:T(2,128)(2,1)S(1)} async-done(((bf16[128,2,2,128]{3,2,1,0:T(2,128)(2,1)}), bf16[128,2,2,128]{3,2,1,0:T(2,128)(2,1)S(1)}, u32[]{:S(2)}, u32[]{:S(2)}) %all-to-all-start.3) | async-done | bytes 131104 | tf_op jit(solution)/shard_map/all_to_all | solution.py:103
  (78 shorter events, 35.4 us)
Async XLA Ops:
  0.0 15.9 %copy-start = (bf16[256,5,128]{2,0,1:T(8,128)(2,1)S(1)}, bf16[256,5,128]{2,0,1:T(8,128)(2,1)}, u32[]{:S(2)}) copy-start(bf16[256,5,128]{2,0,1:T(8,128)(2,1)} %param.16) | copy-start | bytes 983044
  16.5 43.8 %copy-start.3 = (s32[1,7,4,4]{1,3,2,0:T(4,128)S(1)}, s32[1,7,4,4]{1,3,2,0:T(4,128)}, u32[]{:S(2)}) copy-start(s32[1,7,4,4]{1,3,2,0:T(4,128)} %param.21) | copy-start | bytes 1348
  16.5 43.8 %copy-start.4 = (s32[1,7]{1,0:T(1,128)S(1)}, s32[1,7]{1,0:T(1,128)}, u32[]{:S(2)}) copy-start(s32[1,7]{1,0:T(1,128)} %param.20) | copy-start | bytes 88
  19.8 42.5 %collective-permute-start = (bf16[2,256,3,128]{3,1,2,0:T(8,128)(2,1)}, bf16[2,256,3,128]{3,1,2,0:T(8,128)(2,1)S(1)}, u32[]{:S(2)}, u32[]{:S(2)}) collective-permute-start(bf16[2,256,3,128]{3,1,2,0:T(8,128)(2,1)} %pad_maximum_fusion), channel_id=1, source_target_pairs={{0,12},{4,16},{8,20},{12,24},{16,28},{20,32},{24,36},{28,40},{32,4... | collective-permute-start | bytes 1179656 | tf_op jit(solution)/shard_map/ppermute | solution.py:17
  27.3 38.0 %collective-permute-start.1 = (bf16[2,256,3,128]{3,1,2,0:T(8,128)(2,1)}, bf16[2,256,3,128]{3,1,2,0:T(8,128)(2,1)}, u32[]{:S(2)}, u32[]{:S(2)}) collective-permute-start(bf16[2,256,3,128]{3,1,2,0:T(8,128)(2,1)} %pad_maximum_fusion), channel_id=1, source_target_pairs={{0,8},{4,12},{8,16},{12,20},{16,24},{20,28},{24,32},{28,36},{32,40... | collective-permute-start | bytes 1179656 | tf_op jit(solution)/shard_map/ppermute | solution.py:17
  31.6 34.8 %collective-permute-start.2 = (bf16[2,256,3,128]{3,1,2,0:T(8,128)(2,1)}, bf16[2,256,3,128]{3,1,2,0:T(8,128)(2,1)}, u32[]{:S(2)}, u32[]{:S(2)}) collective-permute-start(bf16[2,256,3,128]{3,1,2,0:T(8,128)(2,1)} %pad_maximum_fusion), channel_id=1, source_target_pairs={{0,4},{4,8},{8,12},{12,16},{16,20},{20,24},{24,28},{28,32},{32,36}... | collective-permute-start | bytes 1179656 | tf_op jit(solution)/shard_map/ppermute | solution.py:17
  33.5 34.0 %collective-permute-start.3 = (bf16[2,256,3,128]{3,1,2,0:T(8,128)(2,1)}, bf16[2,256,3,128]{3,1,2,0:T(8,128)(2,1)}, u32[]{:S(2)}, u32[]{:S(2)}) collective-permute-start(bf16[2,256,3,128]{3,1,2,0:T(8,128)(2,1)} %pad_maximum_fusion), channel_id=1, source_target_pairs={{4,0},{8,4},{12,8},{16,12},{20,16},{24,20},{28,24},{32,28},{36,32}... | collective-permute-start | bytes 1179656 | tf_op jit(solution)/shard_map/ppermute | solution.py:17
  36.7 49.5 %collective-permute-start.4 = (bf16[2,256,3,128]{3,1,2,0:T(8,128)(2,1)}, bf16[2,256,3,128]{3,1,2,0:T(8,128)(2,1)}, u32[]{:S(2)}, u32[]{:S(2)}) collective-permute-start(bf16[2,256,3,128]{3,1,2,0:T(8,128)(2,1)} %pad_maximum_fusion), channel_id=1, source_target_pairs={{8,0},{12,4},{16,8},{20,12},{24,16},{28,20},{32,24},{36,28},{40,32... | collective-permute-start | bytes 1179656 | tf_op jit(solution)/shard_map/ppermute | solution.py:17
  41.6 35.6 %all-to-all-start.2 = ((bf16[1,256,2,128]{3,2,0,1:T(2,128)(2,1)}), bf16[1,256,2,128]{3,2,0,1:T(2,128)(2,1)}, u32[]{:S(2)}, u32[]{:S(2)}) async-start(bf16[1,256,2,128]{3,2,0,1:T(2,128)(2,1)} %copy.58), calls=%async_computation.2 | async-start | bytes 262144 | tf_op jit(solution)/shard_map/all_to_all | solution.py:94
  62.3 0.7 copy-start.2
  63.0 24.2 %collective-permute-start.5 = (bf16[2,256,3,128]{3,1,2,0:T(8,128)(2,1)}, bf16[2,256,3,128]{3,1,2,0:T(8,128)(2,1)}, u32[]{:S(2)}, u32[]{:S(2)}) collective-permute-start(bf16[2,256,3,128]{3,1,2,0:T(8,128)(2,1)} %pad_maximum_fusion), channel_id=1, source_target_pairs={{12,0},{16,4},{20,8},{24,12},{28,16},{32,20},{36,24},{40,28},{44,3... | collective-permute-start | bytes 1179656 | tf_op jit(solution)/shard_map/ppermute | solution.py:17
  77.2 26.0 %all-to-all-start.1 = ((bf16[1,256,2,128]{3,2,0,1:T(2,128)(2,1)}), bf16[1,256,2,128]{3,2,0,1:T(2,128)(2,1)}, u32[]{:S(2)}, u32[]{:S(2)}) async-start(bf16[1,256,2,128]{3,2,0,1:T(2,128)(2,1)} %copy.56), calls=%async_computation.1 | async-start | bytes 262144 | tf_op jit(solution)/shard_map/all_to_all | solution.py:93
  88.3 1.6 copy-start.1
  103.2 26.6 %all-to-all-start = ((bf16[1,256,2,128]{3,2,0,1:T(2,128)(2,1)}), bf16[1,256,2,128]{3,2,0,1:T(2,128)(2,1)S(1)}, u32[]{:S(2)}, u32[]{:S(2)}) async-start(bf16[1,256,2,128]{3,2,0,1:T(2,128)(2,1)} %copy.54), calls=%async_computation | async-start | bytes 262144 | tf_op jit(solution)/shard_map/all_to_all | solution.py:95
  132.4 24.8 %all-to-all-start.3 = ((bf16[128,2,2,128]{3,2,1,0:T(2,128)(2,1)}), bf16[128,2,2,128]{3,2,1,0:T(2,128)(2,1)S(1)}, u32[]{:S(2)}, u32[]{:S(2)}) async-start(bf16[128,2,2,128]{3,2,1,0:T(2,128)(2,1)} %copy.64), calls=%async_computation.3 | async-start | bytes 262144 | tf_op jit(solution)/shard_map/all_to_all | solution.py:103
where the time goes:
time: 161 us; the launch traced here: 160 us
  starting transfers between devices  63.6 us (40%)
  waiting for transfers between devices  36.4 us (23%)
  local copies, waits for them, and re-layouts  24.1 us (15%)
  other arithmetic  14.8 us (9%)
  matrix products  10.9 us (7%)
  blocking collectives  9.54 us (6%)
    ppermute x6, starting transfers between devices, shifted(): return lax.ppermute(block, axis, route)  19.4 us
    all_to_all x1, starting transfers between devices, shards(): lax.all_to_all(temp_key, 'ctx', split_axis=1, concat_axis=0, tiled=True)  18.6 us
    all_to_all x1, waiting for transfers between devices, shards(): lax.all_to_all(temp_value, 'ctx', split_axis=1, concat_axis=0, tiled=True)  14.3 us
    psum x1, blocking collectives, shards(): lax.psum((jnp.sum(query_f * query_f, axis=(1, 2)), jnp.sum(key_f * key_f,...  9.54 us
    all_to_all x1, starting transfers between devices, shards(): lax.all_to_all(temp_value, 'ctx', split_axis=1, concat_axis=0, tiled=True)  9.38 us
    all_to_all x1, starting transfers between devices, shards(): lax.all_to_all(temp_query, 'ctx', split_axis=1, concat_axis=0, tiled=True)  8.95 us
    all_to_all x1, waiting for transfers between devices, shards(): lax.all_to_all(temp_key, 'ctx', split_axis=1, concat_axis=0, tiled=True)  8.65 us
    unnamed x15, local copies, waits for them, and re-layouts  7.52 us
  transfers between devices with their start and end apart: 10, of which 4 were waited for; matrix products, arithmetic and copies ran while one was open for 20% of the time, Pallas kernels for 0%

commit v1 on v0

v1 whole, which is shorter than its diff:
```python
import jax
import jax.numpy as jnp
from jax import lax
from jax.experimental import pallas as pl
from jax.experimental.pallas import tpu as pltpu
from jax.sharding import PartitionSpec as P

SIZE = 128
GROUP = 5
TEMP = 2
SPAT = GROUP - TEMP
POS = 256
NB = 7
TILE = 64
NT = 4
FRAMES = 128
HEADS = 20
LOG2E = 1.4426950408889634
SCALE = SIZE ** (-0.5) * LOG2E
UNSEEN = -1e30
BF16 = jnp.bfloat16
F32 = jnp.float32

SUB = POS // FRAMES


def whole(memory_space=pltpu.VMEM):
    return pl.BlockSpec(memory_space=memory_space)


def sorted_heads(class_ref):
    spat, temp = [0] * SPAT, [0] * TEMP
    n_spat, n_temp = 0, 0
    for head in range(GROUP):
        kind = class_ref[head]
        for r in range(SPAT):
            spat[r] = jnp.where((kind == 0) & (n_spat == r), head, spat[r])
        for r in range(TEMP):
            temp[r] = jnp.where((kind != 0) & (n_temp == r), head, temp[r])
        n_spat = n_spat + jnp.where(kind == 0, 1, 0)
        n_temp = n_temp + jnp.where(kind == 0, 0, 1)
    return spat, temp


def sums_kernel(q_ref, k_ref, sums_ref, q_buf, k_buf, sems):
    fetches = []
    for row, (x_ref, x_buf) in enumerate(((q_ref, q_buf), (k_ref, k_buf))):
        for head in range(GROUP):
            fetch = pltpu.make_async_copy(x_ref.at[head], x_buf.at[head], sems.at[row * GROUP + head])
            fetch.start()
            fetches.append(fetch)
    for row, x_buf in enumerate((q_buf, k_buf)):
        total = jnp.zeros((POS, SIZE), F32)
        for head in range(GROUP):
            fetches[row * GROUP + head].wait()
            part = x_buf[head].astype(F32)
            total = total + part * part
        sums_ref[row : row + 1] = jnp.sum(total.T, axis=0, keepdims=True)


def norm_kernel(class_ref, sums_ref, q_gain_ref, k_gain_ref, q_ref, k_ref, v_ref, qs_ref, kvs_ref, chunk_ref):
    spat, temp = sorted_heads(class_ref)
    factors = lax.rsqrt(sums_ref[...] / (HEADS * SIZE) + 1e-06)
    for row, (x_ref, gain_ref) in enumerate(((q_ref, q_gain_ref), (k_ref, k_gain_ref))):
        factor = jnp.broadcast_to(factors[row : row + 1], (SIZE, POS)).T

        def normed(head):
            return (x_ref[head].astype(F32) * factor * gain_ref[pl.ds(head, 1)]).astype(BF16)

        for r in range(TEMP):
            chunk_ref[:, row * TEMP + r] = normed(temp[r]).reshape(FRAMES, SUB, SIZE)
        for r in range(SPAT):
            if row == 0:
                qs_ref[r] = normed(spat[r])
            else:
                kvs_ref[0, r] = normed(spat[r])
    for r in range(TEMP):
        chunk_ref[:, 2 * TEMP + r] = v_ref[temp[r]].reshape(FRAMES, SUB, SIZE)
    for r in range(SPAT):
        kvs_ref[1, r] = v_ref[spat[r]]


def dot_t(a, b):
    return lax.dot_general(a, b, (((1,), (1,)), ((), ())), preferred_element_type=F32)


def attend(q, blocks, scores_ref, bias_of):
    top = None
    for w, (k, _) in enumerate(blocks):
        scores = bias_of(w, dot_t(q, k()) * SCALE)
        scores_ref[w] = scores
        block_top = jnp.maximum(scores[:, :SIZE], scores[:, SIZE:])
        top = block_top if top is None else jnp.maximum(top, block_top)
    top = jnp.max(top, axis=1, keepdims=True)
    total = jnp.zeros((POS, SIZE), F32)
    out = jnp.zeros((POS, SIZE), F32)
    for w, (_, v) in enumerate(blocks):
        expo = jnp.exp2(scores_ref[w] - top)
        total = total + expo[:, :SIZE] + expo[:, SIZE:]
        out = out + jnp.dot(expo.astype(BF16), v(), preferred_element_type=F32)
    return (out / jnp.sum(total, axis=1, keepdims=True)).astype(BF16)


def temporal_kernel(x_ref, y_ref):
    query_row = lax.broadcasted_iota(jnp.int32, (POS, POS), 0) % SUB
    key_row = lax.broadcasted_iota(jnp.int32, (POS, POS), 1) % SUB
    bias = jnp.where(query_row == key_row, 0.0, UNSEEN)
    for head in range(TEMP):
        q, k, v = (x_ref[:, t * TEMP + head].reshape(POS, SIZE) for t in range(3))
        scores = dot_t(q, k) * SCALE + bias
        expo = jnp.exp2(scores - jnp.max(scores, axis=1, keepdims=True))
        total = jnp.sum(expo, axis=1, keepdims=True)
        out = jnp.dot(expo.astype(BF16), v, preferred_element_type=F32) / total
        y_ref[:, head] = out.astype(BF16).reshape(FRAMES, SUB, SIZE)


def spatial_kernel(order_ref, bias_ref, q_ref, *refs):
    kv_refs, out_ref, scores_ref = refs[:NB], refs[NB], refs[NB + 1]

    def bias_of(w, scores):
        tiles = [
            scores[a * TILE : (a + 1) * TILE] + bias_ref[a : a + 1, w * POS : (w + 1) * POS] for a in range(NT)
        ]
        return jnp.concatenate(tiles, axis=0)

    blocks = [(lambda ref=ref: ref[0, 0], lambda ref=ref: ref[1, 0]) for ref in kv_refs]
    out_ref[0] = attend(q_ref[0], blocks, scores_ref, bias_of)


def join_kernel(order_ref, rows_ref, spatial_ref, out_ref):
    out_ref[0] = rows_ref[:, 0].reshape(POS, SIZE)


def route(block, target):
    pairs = [(i, target(i)) for i in range(FRAMES) if 0 <= target(i) < FRAMES]
    return lax.ppermute(block, "ctx", pairs)


def first_window(own):
    below = route(own, lambda i: i + 2)
    above = route(own, lambda i: i - 2)
    twin = route(own, lambda i: i ^ 1)
    return below, above, twin


def rest_window(own, below, above, twin):
    passed = jnp.where(lax.axis_index("ctx") % 2 == 1, below, above)
    far = route(passed, lambda i: i + 1 if i % 2 else i - 1)
    return [far, below, route(below, lambda i: i ^ 1), own, twin, above, route(above, lambda i: i ^ 1)]


EVEN = (-3, -2, -1, 0, 1, 2, 3)
ODD = (3, -2, -3, 0, -1, 2, 1)


def bias_rows(neighbours, tiles):
    frame = lax.axis_index("ctx")
    offsets = jnp.where(frame % 2 == 0, jnp.array(EVEN, jnp.int32), jnp.array(ODD, jnp.int32))
    listed = (neighbours[0][None, :] == (frame + offsets)[:, None]).astype(jnp.int32)
    times = jnp.sum(listed[:, :, None, None] * tiles[0][None], axis=1)
    bias = jnp.where(times > 0, jnp.log2(jnp.maximum(times, 1).astype(F32)), UNSEEN)
    bias = jnp.repeat(jnp.transpose(bias, (1, 0, 2)), TILE, axis=2)
    return bias.reshape(NT, NB * POS)


def head_order(head_class):
    heads = jnp.arange(GROUP, dtype=jnp.int32)
    rank_key = head_class * GROUP + heads
    rank = jnp.sum((rank_key[None, :] < rank_key[:, None]).astype(jnp.int32), axis=1)
    return jnp.sum(jnp.where(rank[:, None] == heads[None, :], heads[:, None], 0), axis=0)


def bf16(*dims):
    return jax.ShapeDtypeStruct(dims, BF16)


def params(mib=32):
    return pltpu.CompilerParams(vmem_limit_bytes=mib * 1024 * 1024)


def swap_all(block):
    return lax.all_to_all(block, "ctx", split_axis=0, concat_axis=0, tiled=True)


def shards(query, key, value, query_gain, key_gain, head_class, neighbours, tiles):
    q, k, v = (jnp.transpose(a, (1, 0, 2)) for a in (query, key, value))
    sums = pl.pallas_call(
        sums_kernel,
        out_shape=jax.ShapeDtypeStruct((2, POS), F32),
        in_specs=[whole(pl.ANY)] * 2,
        out_specs=whole(),
        scratch_shapes=[
            pltpu.VMEM((GROUP, POS, SIZE), BF16),
            pltpu.VMEM((GROUP, POS, SIZE), BF16),
            pltpu.SemaphoreType.DMA((2 * GROUP,)),
        ],
        compiler_params=params(60),
        name="sums",
    )(q, k)
    sums = lax.psum(sums, "head")
    q_own, kv_own, chunk = pl.pallas_call(
        norm_kernel,
        out_shape=(
            bf16(SPAT, POS, SIZE),
            bf16(2, SPAT, POS, SIZE),
            bf16(FRAMES, 3 * TEMP, SUB, SIZE),
        ),
        in_specs=[whole(pltpu.SMEM)] + [whole()] * 6,
        out_specs=(whole(),) * 3,
        compiler_params=params(16),
        name="norm",
    )(head_class, sums, query_gain, key_gain, q, k, v)
    rows = swap_all(chunk)
    first = first_window(kv_own)
    outputs = pl.pallas_call(
        temporal_kernel,
        out_shape=bf16(FRAMES, TEMP, SUB, SIZE),
        in_specs=[whole()],
        out_specs=whole(),
        compiler_params=params(16),
        name="temporal",
    )(rows)
    outputs, first = lax.optimization_barrier((outputs, first))
    temporal_out = swap_all(outputs)
    window = rest_window(kv_own, *first)

    order = head_order(head_class)
    bias = bias_rows(neighbours, tiles)
    head_block = pl.BlockSpec((1, POS, SIZE), lambda h, order_ref: (h, 0, 0))
    spatial = pl.pallas_call(
        spatial_kernel,
        out_shape=bf16(GROUP, POS, SIZE),
        grid_spec=pltpu.PrefetchScalarGridSpec(
            num_scalar_prefetch=1,
            grid=(SPAT,),
            in_specs=[pl.BlockSpec((NT, NB * POS), lambda h, order_ref: (0, 0))] + [head_block]
            + [pl.BlockSpec((2, 1, POS, SIZE), lambda h, order_ref: (0, h, 0, 0))] * NB,
            out_specs=pl.BlockSpec((1, POS, SIZE), lambda h, order_ref: (order_ref[h], 0, 0)),
            scratch_shapes=[pltpu.VMEM((NB, POS, POS), F32)],
        ),
        compiler_params=params(),
        name="spatial",
    )(order, bias, q_own, *window)
    out = pl.pallas_call(
        join_kernel,
        out_shape=bf16(GROUP, POS, SIZE),
        grid_spec=pltpu.PrefetchScalarGridSpec(
            num_scalar_prefetch=1,
            grid=(TEMP,),
            in_specs=[
                pl.BlockSpec((FRAMES, 1, SUB, SIZE), lambda h, order_ref: (0, h, 0, 0)),
                pl.BlockSpec(memory_space=pl.ANY),
            ],
            out_specs=pl.BlockSpec((1, POS, SIZE), lambda h, order_ref: (order_ref[SPAT + h], 0, 0)),
        ),
        input_output_aliases={2: 0},
        compiler_params=params(),
        name="join",
    )(order, temporal_out, spatial)
    return jnp.transpose(out, (1, 0, 2))


def solution(mesh):
    in_specs = (
        P("ctx", "head", None),
        P("ctx", "head", None),
        P("ctx", "head", None),
        P("head", None),
        P("head", None),
        P("head"),
        P("ctx", None),
        P("ctx", None, None, None),
    )
    out_specs = P("ctx", "head", None)
    return jax.shard_map(shards, mesh=mesh, in_specs=in_specs, out_specs=out_specs, check_vma=False)
```

time: 161 us -> 102 us (0.63)
  local copies, waits for them, and re-layouts: 24.1 us -> 3.14 us
  other arithmetic: 14.8 us -> 0.98 us
  starting transfers between devices: 63.6 us -> 50.7 us
  waiting for transfers between devices: 36.4 us -> 24.3 us
  Pallas kernels: 0 us -> 11.1 us
  matrix products: 10.9 us -> 0 us
    all_to_all x4 -> x2, waiting for transfers between devices: 36.4 us -> 18.2 us  [swap_all(): return lax.all_to_all(block, 'ctx', split_axis=0, concat_axis=0, tiled=True)]
    pallas_call x0 -> x5, Pallas kernels: none -> 11.1 us  [the longest x1 4.66 us: shards(): pl.pallas_call(spatial_kernel, out_shape=bf16(GROUP, POS, SIZE), grid_spe...]
    dot_general x8 -> x0, matrix products: 9.65 us -> none  [the longest x3 4.16 us: head_block(): jnp.einsum('fqd,fkd->fqk', q_head, k_head, preferred_element_type=jnp.flo...]
    all_to_all x4 -> x2, starting transfers between devices: 44.2 us -> 34.7 us  [swap_all(): return lax.all_to_all(block, 'ctx', split_axis=0, concat_axis=0, tiled=True)]
    gather x8 -> x0, local copies, waits for them, and re-layouts: 6.58 us -> none  [the longest x1 2.5 us: shards(): jnp.take(window, local_frames, axis=1)]
    ppermute x6, waiting for transfers between devices: 0.02 us -> 6.15 us  [route(): return lax.ppermute(block, 'ctx', pairs)]
    unnamed x15 -> x20, local copies, waits for them, and re-layouts: 7.52 us -> 2.95 us
    reshape x4 -> x0, local copies, waits for them, and re-layouts: 4.29 us -> none  [the longest x1 1.95 us: shards(): window.reshape(2, (2 * hops + 1) * frames_dev, FRAME_POS, n_spatial, size)]
  transfers between devices with their start and end apart: 10 -> 8, of which waited for: 4 -> 2; matrix products, arithmetic and copies ran while one was open for 20% -> 1% of each run, Pallas kernels for 0% -> 6%
where the time goes in v1:
time: 102 us; the launch traced here: 100 us
  starting transfers between devices  50.7 us (50%)
  waiting for transfers between devices  24.3 us (24%)
  Pallas kernels  11.1 us (11%)
  blocking collectives  9.69 us (10%)
  local copies, waits for them, and re-layouts  3.14 us (3%)
    all_to_all x2, starting transfers between devices, swap_all(): return lax.all_to_all(block, 'ctx', split_axis=0, concat_axis=0, tiled=True)  34.7 us
    all_to_all x2, waiting for transfers between devices, swap_all(): return lax.all_to_all(block, 'ctx', split_axis=0, concat_axis=0, tiled=True)  18.2 us
    ppermute x6, starting transfers between devices, route(): return lax.ppermute(block, 'ctx', pairs)  16 us
    psum x1, blocking collectives, shards(): sums = lax.psum(sums, 'head')  9.69 us
    ppermute x6, waiting for transfers between devices, route(): return lax.ppermute(block, 'ctx', pairs)  6.15 us
    pallas_call x1, Pallas kernels, shards(): pl.pallas_call(spatial_kernel, out_shape=bf16(GROUP, POS, SIZE), grid_spe...  4.66 us
    unnamed x20, local copies, waits for them, and re-layouts  2.95 us
  transfers between devices with their start and end apart: 8, of which 2 were waited for; matrix products, arithmetic and copies ran while one was open for 1% of the time, Pallas kernels for 6%

profile of v1, /device:TPU:1, one launch (start us, length us, event | category | flops | bytes accessed | tf_op | source)
XLA Modules:
  0.0 100.1 jit_solution(16490046307076975328)
XLA Ops:
  0.0 2.0 %sums.1 = f32[2,256]{1,0:T(2,128)} custom-call(bf16[5,256,128]{2,1,0:T(8,128)(2,1)} %bitcast.8, bf16[5,256,128]{2,1,0:T(8,128)(2,1)} %bitcast.10), custom_call_target="tpu_custom_call" | custom-call | tf_op jit(solution)/shard_map/sums/pallas_call | solution.py:187
  2.0 9.7 %psum.7.sums_ref = f32[2,256]{1,0:T(2,128)S(1)} all-reduce(f32[2,256]{1,0:T(2,128)} %sums.1), channel_id=1, replica_groups=mesh['ctx'=128,'head'=4] {'head'}, use_global_device_ids=true, to_apply=%region_2.3 | all-reduce | flops 512 | bytes 4096 | tf_op jit(solution)/shard_map/psum | solution.py:200
  11.7 0.6 copy-done.5
  12.3 1.0 copy-done.2
  13.3 0.7 copy-done.4
  14.0 1.7 %norm.1 = (bf16[3,256,128]{2,1,0:T(8,128)(2,1)S(1)}, bf16[2,3,256,128]{3,2,1,0:T(8,128)(2,1)S(1)}, bf16[128,6,2,128]{3,2,1,0:T(2,128)(2,1)}) custom-call(s32[5]{0:T(128)S(1)} %copy-done.5, f32[2,256]{1,0:T(2,128)S(1)} %psum.7.sums_ref, f32[5,128]{1,0:T(8,128)S(1)} %copy-done.3, f32[5,128]{1,0:T(8,128)S(1)} %copy-done.4, bf16[5,256,128]{2,1,0:T(8,128)(2,1)S(1)} %bitcast.9, ...), custom_call_target="tpu_custom_call" | custom-call | tf_op jit(solution)/shard_map/norm/pallas_call | solution.py:201
  15.7 21.6 %all-to-all-start = ((bf16[128,6,2,128]{3,2,1,0:T(2,128)(2,1)}), bf16[128,6,2,128]{3,2,1,0:T(2,128)(2,1)S(1)}, u32[]{:S(2)}, u32[]{:S(2)}) async-start(bf16[128,6,2,128]{3,2,1,0:T(2,128)(2,1)} %get-tuple-element.12), calls=%async_computation | async-start | bytes 786432 | tf_op jit(solution)/shard_map/all_to_all | solution.py:182
  37.3 2.8 %collective-permute-start.2 = (bf16[2,3,256,128]{3,2,1,0:T(8,128)(2,1)S(1)}, bf16[2,3,256,128]{3,2,1,0:T(8,128)(2,1)S(1)}, u32[]{:S(2)}, u32[]{:S(2)}) collective-permute-start(bf16[2,3,256,128]{3,2,1,0:T(8,128)(2,1)S(1)} %get-tuple-element.13.refs_3_), channel_id=1, source_target_pairs={{0,4},{4,0},{8,12},{12,8},{16,20},{20,16},{24,28},{28,24},{32,36},... | collective-permute-start | bytes 1179656 | tf_op jit(solution)/shard_map/ppermute | solution.py:136
  40.1 1.3 %collective-permute-start.1 = (bf16[2,3,256,128]{3,2,1,0:T(8,128)(2,1)S(1)}, bf16[2,3,256,128]{3,2,1,0:T(8,128)(2,1)S(1)}, u32[]{:S(2)}, u32[]{:S(2)}) collective-permute-start(bf16[2,3,256,128]{3,2,1,0:T(8,128)(2,1)S(1)} %get-tuple-element.13.refs_3_), channel_id=1, source_target_pairs={{8,0},{12,4},{16,8},{20,12},{24,16},{28,20},{32,24},{36,28},{40,32... | collective-permute-start | bytes 1179656 | tf_op jit(solution)/shard_map/ppermute | solution.py:136
  41.4 4.0 %collective-permute-start = (bf16[2,3,256,128]{3,2,1,0:T(8,128)(2,1)S(1)}, bf16[2,3,256,128]{3,2,1,0:T(8,128)(2,1)S(1)}, u32[]{:S(2)}, u32[]{:S(2)}) collective-permute-start(bf16[2,3,256,128]{3,2,1,0:T(8,128)(2,1)S(1)} %get-tuple-element.13.refs_3_), channel_id=1, source_target_pairs={{0,8},{4,12},{8,16},{12,20},{16,24},{20,28},{24,32},{28,36},{32,40... | collective-permute-start | bytes 1179656 | tf_op jit(solution)/shard_map/ppermute | solution.py:136
  45.5 0.6 copy-done.8
  46.2 0.6 multiply_reduce_fusion
  46.9 0.1 reshape_reshape.3.bias_ref
  47.0 18.2 %all-to-all-done.x_ref = bf16[128,6,2,128]{3,2,1,0:T(2,128)(2,1)S(1)} async-done(((bf16[128,6,2,128]{3,2,1,0:T(2,128)(2,1)}), bf16[128,6,2,128]{3,2,1,0:T(2,128)(2,1)S(1)}, u32[]{:S(2)}, u32[]{:S(2)}) %all-to-all-start) | async-done | bytes 393248 | tf_op jit(solution)/shard_map/all_to_all | solution.py:182
  65.2 1.4 %temporal.1 = bf16[128,2,2,128]{3,2,1,0:T(2,128)(2,1)} custom-call(bf16[128,6,2,128]{3,2,1,0:T(2,128)(2,1)S(1)} %all-to-all-done.x_ref), custom_call_target="tpu_custom_call" | custom-call | tf_op jit(solution)/shard_map/temporal/pallas_call | solution.py:215
  66.6 13.1 %all-to-all-start.1 = ((bf16[128,2,2,128]{3,2,1,0:T(2,128)(2,1)}), bf16[128,2,2,128]{3,2,1,0:T(2,128)(2,1)S(1)}, u32[]{:S(2)}, u32[]{:S(2)}) async-start(bf16[128,2,2,128]{3,2,1,0:T(2,128)(2,1)} %temporal.1), calls=%async_computation.1 | async-start | bytes 262144 | tf_op jit(solution)/shard_map/all_to_all | solution.py:182
  79.7 2.8 %collective-permute-start.4 = (bf16[2,3,256,128]{3,2,1,0:T(8,128)(2,1)S(1)}, bf16[2,3,256,128]{3,2,1,0:T(8,128)(2,1)S(1)}, u32[]{:S(2)}, u32[]{:S(2)}) collective-permute-start(bf16[2,3,256,128]{3,2,1,0:T(8,128)(2,1)S(1)} %collective-permute-done.refs_1_), channel_id=1, source_target_pairs={{0,4},{4,0},{8,12},{12,8},{16,20},{20,16},{24,28},{28,24},{32,36},... | collective-permute-start | bytes 1179656 | tf_op jit(solution)/shard_map/ppermute | solution.py:136
  82.5 1.9 %collective-permute-start.5 = (bf16[2,3,256,128]{3,2,1,0:T(8,128)(2,1)S(1)}, bf16[2,3,256,128]{3,2,1,0:T(8,128)(2,1)S(1)}, u32[]{:S(2)}, u32[]{:S(2)}) collective-permute-start(bf16[2,3,256,128]{3,2,1,0:T(8,128)(2,1)S(1)} %collective-permute-done.1.refs_5_), channel_id=1, source_target_pairs={{0,4},{4,0},{8,12},{12,8},{16,20},{20,16},{24,28},{28,24},{32,36},... | collective-permute-start | bytes 1179656 | tf_op jit(solution)/shard_map/ppermute | solution.py:136
  84.5 3.1 %collective-permute-start.3 = (bf16[2,3,256,128]{3,2,1,0:T(8,128)(2,1)S(1)}, bf16[2,3,256,128]{3,2,1,0:T(8,128)(2,1)S(1)}, u32[]{:S(2)}, u32[]{:S(2)}) collective-permute-start(bf16[2,3,256,128]{3,2,1,0:T(8,128)(2,1)S(1)} %broadcast_select_fusion), channel_id=1, source_target_pairs={{4,8},{8,4},{12,16},{16,12},{20,24},{24,20},{28,32},{32,28},{36,40... | collective-permute-start | bytes 1179656 | tf_op jit(solution)/shard_map/ppermute | solution.py:136
  87.7 0.2 convert_reduce_fusion
  87.8 0.1 select_reduce_fusion.order_ref
  87.9 6.1 %collective-permute-done.3.refs_0_ = bf16[2,3,256,128]{3,2,1,0:T(8,128)(2,1)S(1)} collective-permute-done((bf16[2,3,256,128]{3,2,1,0:T(8,128)(2,1)S(1)}, bf16[2,3,256,128]{3,2,1,0:T(8,128)(2,1)S(1)}, u32[]{:S(2)}, u32[]{:S(2)}) %collective-permute-start.3) | collective-permute-done | bytes 393248 | tf_op jit(solution)/shard_map/ppermute | solution.py:136
  94.1 4.7 %spatial.1.spatial_ref = bf16[5,256,128]{2,1,0:T(8,128)(2,1)} custom-call(s32[5]{0:T(128)S(1)} %select_reduce_fusion.order_ref, f32[4,1792]{1,0:T(4,128)S(1)} %reshape_reshape.3.bias_ref, bf16[3,256,128]{2,1,0:T(8,128)(2,1)S(1)} %get-tuple-element.15.q_ref, bf16[2,3,256,128]{3,2,1,0:T(8,128)(2,1)S(1)} %collective-permute-done.3.refs_0_, ...), custom_call_target="tpu_custom_call" | custom-call | tf_op jit(solution)/shard_map/spatial/pallas_call | solution.py:230
  98.7 1.4 %join.1 = bf16[5,256,128]{2,1,0:T(8,128)(2,1)} custom-call(s32[5]{0:T(128)S(1)} %select_reduce_fusion.order_ref, bf16[128,2,2,128]{3,2,1,0:T(2,128)(2,1)S(1)} %all-to-all-done.1.rows_ref, bf16[5,256,128]{2,1,0:T(8,128)(2,1)} %spatial.1.spatial_ref), custom_call_target="tpu_custom_call", output_to_operand_aliasing={{}: (2, {})} | custom-call | tf_op jit(solution)/shard_map/join/pallas_call | solution.py:244
  (29 shorter events, 0.3 us)
Async XLA Ops:
  0.0 11.7 %copy-start = (bf16[256,5,128]{2,0,1:T(8,128)(2,1)S(1)}, bf16[256,5,128]{2,0,1:T(8,128)(2,1)}, u32[]{:S(2)}) copy-start(bf16[256,5,128]{2,0,1:T(8,128)(2,1)} %param.10) | copy-start | bytes 983044
  0.0 11.7 %copy-start.1 = (bf16[256,5,128]{2,0,1:T(8,128)(2,1)S(1)}, bf16[256,5,128]{2,0,1:T(8,128)(2,1)}, u32[]{:S(2)}) copy-start(bf16[256,5,128]{2,0,1:T(8,128)(2,1)} %param.11) | copy-start | bytes 983044
  2.0 9.7 %copy-start.3 = (f32[5,128]{1,0:T(8,128)S(1)}, f32[5,128]{1,0:T(8,128)}, u32[]{:S(2)}) copy-start(f32[5,128]{1,0:T(8,128)} %q_gain_ref.1) | copy-start | bytes 7684
  11.7 0.7 copy-start.5
  12.3 1.0 copy-start.2
  13.3 0.7 copy-start.4
  15.7 49.5 %all-to-all-start = ((bf16[128,6,2,128]{3,2,1,0:T(2,128)(2,1)}), bf16[128,6,2,128]{3,2,1,0:T(2,128)(2,1)S(1)}, u32[]{:S(2)}, u32[]{:S(2)}) async-start(bf16[128,6,2,128]{3,2,1,0:T(2,128)(2,1)} %get-tuple-element.12), calls=%async_computation | async-start | bytes 786432 | tf_op jit(solution)/shard_map/all_to_all | solution.py:182
  37.3 29.2 %collective-permute-start.2 = (bf16[2,3,256,128]{3,2,1,0:T(8,128)(2,1)S(1)}, bf16[2,3,256,128]{3,2,1,0:T(8,128)(2,1)S(1)}, u32[]{:S(2)}, u32[]{:S(2)}) collective-permute-start(bf16[2,3,256,128]{3,2,1,0:T(8,128)(2,1)S(1)} %get-tuple-element.13.refs_3_), channel_id=1, source_target_pairs={{0,4},{4,0},{8,12},{12,8},{16,20},{20,16},{24,28},{28,24},{32,36},... | collective-permute-start | bytes 1179656 | tf_op jit(solution)/shard_map/ppermute | solution.py:136
  40.1 26.4 %collective-permute-start.1 = (bf16[2,3,256,128]{3,2,1,0:T(8,128)(2,1)S(1)}, bf16[2,3,256,128]{3,2,1,0:T(8,128)(2,1)S(1)}, u32[]{:S(2)}, u32[]{:S(2)}) collective-permute-start(bf16[2,3,256,128]{3,2,1,0:T(8,128)(2,1)S(1)} %get-tuple-element.13.refs_3_), channel_id=1, source_target_pairs={{8,0},{12,4},{16,8},{20,12},{24,16},{28,20},{32,24},{36,28},{40,32... | collective-permute-start | bytes 1179656 | tf_op jit(solution)/shard_map/ppermute | solution.py:136
  41.4 25.1 %collective-permute-start = (bf16[2,3,256,128]{3,2,1,0:T(8,128)(2,1)S(1)}, bf16[2,3,256,128]{3,2,1,0:T(8,128)(2,1)S(1)}, u32[]{:S(2)}, u32[]{:S(2)}) collective-permute-start(bf16[2,3,256,128]{3,2,1,0:T(8,128)(2,1)S(1)} %get-tuple-element.13.refs_3_), channel_id=1, source_target_pairs={{0,8},{4,12},{8,16},{12,20},{16,24},{20,28},{24,32},{28,36},{32,40... | collective-permute-start | bytes 1179656 | tf_op jit(solution)/shard_map/ppermute | solution.py:136
  45.5 0.7 copy-start.8
  45.5 0.7 copy-start.9
  45.5 0.7 copy-start.7
  45.5 0.7 copy-start.6
  66.6 32.2 %all-to-all-start.1 = ((bf16[128,2,2,128]{3,2,1,0:T(2,128)(2,1)}), bf16[128,2,2,128]{3,2,1,0:T(2,128)(2,1)S(1)}, u32[]{:S(2)}, u32[]{:S(2)}) async-start(bf16[128,2,2,128]{3,2,1,0:T(2,128)(2,1)} %temporal.1), calls=%async_computation.1 | async-start | bytes 262144 | tf_op jit(solution)/shard_map/all_to_all | solution.py:182
  79.7 14.4 %collective-permute-start.4 = (bf16[2,3,256,128]{3,2,1,0:T(8,128)(2,1)S(1)}, bf16[2,3,256,128]{3,2,1,0:T(8,128)(2,1)S(1)}, u32[]{:S(2)}, u32[]{:S(2)}) collective-permute-start(bf16[2,3,256,128]{3,2,1,0:T(8,128)(2,1)S(1)} %collective-permute-done.refs_1_), channel_id=1, source_target_pairs={{0,4},{4,0},{8,12},{12,8},{16,20},{20,16},{24,28},{28,24},{32,36},... | collective-permute-start | bytes 1179656 | tf_op jit(solution)/shard_map/ppermute | solution.py:136
  82.5 11.6 %collective-permute-start.5 = (bf16[2,3,256,128]{3,2,1,0:T(8,128)(2,1)S(1)}, bf16[2,3,256,128]{3,2,1,0:T(8,128)(2,1)S(1)}, u32[]{:S(2)}, u32[]{:S(2)}) collective-permute-start(bf16[2,3,256,128]{3,2,1,0:T(8,128)(2,1)S(1)} %collective-permute-done.1.refs_5_), channel_id=1, source_target_pairs={{0,4},{4,0},{8,12},{12,8},{16,20},{20,16},{24,28},{28,24},{32,36},... | collective-permute-start | bytes 1179656 | tf_op jit(solution)/shard_map/ppermute | solution.py:136
  84.5 9.6 %collective-permute-start.3 = (bf16[2,3,256,128]{3,2,1,0:T(8,128)(2,1)S(1)}, bf16[2,3,256,128]{3,2,1,0:T(8,128)(2,1)S(1)}, u32[]{:S(2)}, u32[]{:S(2)}) collective-permute-start(bf16[2,3,256,128]{3,2,1,0:T(8,128)(2,1)S(1)} %broadcast_select_fusion), channel_id=1, source_target_pairs={{4,8},{8,4},{12,16},{16,12},{20,24},{24,20},{28,32},{32,28},{36,40... | collective-permute-start | bytes 1179656 | tf_op jit(solution)/shard_map/ppermute | solution.py:136

commit v2 on v1

--- a/solution.py
+++ b/solution.py
@@ -58,26 +58,41 @@
         sums_ref[row : row + 1] = jnp.sum(total.T, axis=0, keepdims=True)
 
 
-def norm_kernel(class_ref, sums_ref, q_gain_ref, k_gain_ref, q_ref, k_ref, v_ref, qs_ref, kvs_ref, chunk_ref):
+def fetched(refs, heads, buf_ref, sems):
+    fetches = []
+    for t, x_ref in enumerate(refs):
+        for r, head in enumerate(heads):
+            place = t * len(heads) + r
+            fetches.append(pltpu.make_async_copy(x_ref.at[head], buf_ref.at[place], sems.at[place]))
+            fetches[-1].start()
+    return fetches
+
+
+def factors_of(sums_ref):
+    factors = lax.rsqrt(sums_ref[...] / (HEADS * SIZE) + 1e-06)
+    return [jnp.broadcast_to(factors[row : row + 1], (SIZE, POS)).T for row in range(2)]
+
+
+def norm_kernel(
+    class_ref, sums_ref, q_gain_ref, k_gain_ref, q_ref, k_ref, v_ref, qs_ref, kvs_ref, chunk_ref, buf_ref, sems
+):
     spat, temp = sorted_heads(class_ref)
-    factors = lax.rsqrt(sums_ref[...] / (HEADS * SIZE) + 1e-06)
-    for row, (x_ref, gain_ref) in enumerate(((q_ref, q_gain_ref), (k_ref, k_gain_ref))):
-        factor = jnp.broadcast_to(factors[row : row + 1], (SIZE, POS)).T
-
-        def normed(head):
-            return (x_ref[head].astype(F32) * factor * gain_ref[pl.ds(head, 1)]).astype(BF16)
-
-        for r in range(TEMP):
-            chunk_ref[:, row * TEMP + r] = normed(temp[r]).reshape(FRAMES, SUB, SIZE)
-        for r in range(SPAT):
-            if row == 0:
-                qs_ref[r] = normed(spat[r])
-            else:
-                kvs_ref[0, r] = normed(spat[r])
-    for r in range(TEMP):
-        chunk_ref[:, 2 * TEMP + r] = v_ref[temp[r]].reshape(FRAMES, SUB, SIZE)
-    for r in range(SPAT):
-        kvs_ref[1, r] = v_ref[spat[r]]
+    heads = spat + temp
+    fetches = fetched((k_ref, v_ref, q_ref), heads, buf_ref, sems)
+    factors = factors_of(sums_ref)
+    for place, fetch in enumerate(fetches):
+        t, r = divmod(place, GROUP)
+        fetch.wait()
+        rows = buf_ref[place]
+        if t != 1:
+            gain = (k_gain_ref, None, q_gain_ref)[t][pl.ds(heads[r], 1)]
+            rows = (rows.astype(F32) * factors[1 - t // 2] * gain).astype(BF16)
+        if r >= SPAT:
+            chunk_ref[:, (1, 2, 0)[t] * TEMP + r - SPAT] = rows.reshape(FRAMES, SUB, SIZE)
+        elif t < 2:
+            kvs_ref[t, r] = rows
+        else:
+            qs_ref[r] = rows
 
 
 def dot_t(a, b):
@@ -115,7 +130,7 @@
 
 
 def spatial_kernel(order_ref, bias_ref, q_ref, *refs):
-    kv_refs, out_ref, scores_ref = refs[:NB], refs[NB], refs[NB + 1]
+    kv_refs, (out_ref, scores_ref, rows_ref, sems) = refs[:NB], refs[NB:]
 
     def bias_of(w, scores):
         tiles = [
@@ -123,12 +138,25 @@
         ]
         return jnp.concatenate(tiles, axis=0)
 
-    blocks = [(lambda ref=ref: ref[0, 0], lambda ref=ref: ref[1, 0]) for ref in kv_refs]
-    out_ref[0] = attend(q_ref[0], blocks, scores_ref, bias_of)
-
-
-def join_kernel(order_ref, rows_ref, spatial_ref, out_ref):
-    out_ref[0] = rows_ref[:, 0].reshape(POS, SIZE)
+    copies = []
+    for head in range(SPAT):
+        blocks = [(lambda ref=ref: ref[0, head], lambda ref=ref: ref[1, head]) for ref in kv_refs]
+        rows_ref[head] = attend(q_ref[head], blocks, scores_ref, bias_of)
+        copies.append(pltpu.make_async_copy(rows_ref.at[head], out_ref.at[order_ref[head]], sems.at[head]))
+        copies[-1].start()
+    for copy in copies:
+        copy.wait()
+
+
+def join_kernel(order_ref, moved_ref, spatial_ref, out_ref, rows_ref, sems):
+    copies = []
+    for head in range(TEMP):
+        rows_ref[head] = moved_ref[:, head].reshape(POS, SIZE)
+        place = order_ref[SPAT + head]
+        copies.append(pltpu.make_async_copy(rows_ref.at[head], out_ref.at[place], sems.at[head]))
+        copies[-1].start()
+    for copy in copies:
+        copy.wait()
 
 
 def route(block, target):
@@ -145,6 +173,7 @@
 
 def rest_window(own, below, above, twin):
     passed = jnp.where(lax.axis_index("ctx") % 2 == 1, below, above)
+    passed, below, above = lax.optimization_barrier((passed, below, above))
     far = route(passed, lambda i: i + 1 if i % 2 else i - 1)
     return [far, below, route(below, lambda i: i ^ 1), own, twin, above, route(above, lambda i: i ^ 1)]
 
@@ -205,9 +234,10 @@
             bf16(2, SPAT, POS, SIZE),
             bf16(FRAMES, 3 * TEMP, SUB, SIZE),
         ),
-        in_specs=[whole(pltpu.SMEM)] + [whole()] * 6,
+        in_specs=[whole(pltpu.SMEM)] + [whole()] * 3 + [whole(pl.ANY)] * 3,
         out_specs=(whole(),) * 3,
-        compiler_params=params(16),
+        scratch_shapes=[pltpu.VMEM((3 * GROUP, POS, SIZE), BF16), pltpu.SemaphoreType.DMA((3 * GROUP,))],
+        compiler_params=params(60),
         name="norm",
     )(head_class, sums, query_gain, key_gain, q, k, v)
     rows = swap_all(chunk)
@@ -226,35 +256,28 @@
 
     order = head_order(head_class)
     bias = bias_rows(neighbours, tiles)
-    head_block = pl.BlockSpec((1, POS, SIZE), lambda h, order_ref: (h, 0, 0))
+    smem = whole(pltpu.SMEM)
     spatial = pl.pallas_call(
         spatial_kernel,
         out_shape=bf16(GROUP, POS, SIZE),
-        grid_spec=pltpu.PrefetchScalarGridSpec(
-            num_scalar_prefetch=1,
-            grid=(SPAT,),
-            in_specs=[pl.BlockSpec((NT, NB * POS), lambda h, order_ref: (0, 0))] + [head_block]
-            + [pl.BlockSpec((2, 1, POS, SIZE), lambda h, order_ref: (0, h, 0, 0))] * NB,
-            out_specs=pl.BlockSpec((1, POS, SIZE), lambda h, order_ref: (order_ref[h], 0, 0)),
-            scratch_shapes=[pltpu.VMEM((NB, POS, POS), F32)],
-        ),
-        compiler_params=params(),
+        in_specs=[smem] + [whole()] * (2 + NB),
+        out_specs=whole(pl.ANY),
+        scratch_shapes=[
+            pltpu.VMEM((NB, POS, POS), F32),
+            pltpu.VMEM((SPAT, POS, SIZE), BF16),
+            pltpu.SemaphoreType.DMA((SPAT,)),
+        ],
+        compiler_params=params(16),
         name="spatial",
     )(order, bias, q_own, *window)
     out = pl.pallas_call(
         join_kernel,
         out_shape=bf16(GROUP, POS, SIZE),
-        grid_spec=pltpu.PrefetchScalarGridSpec(
-            num_scalar_prefetch=1,
-            grid=(TEMP,),
-            in_specs=[
-                pl.BlockSpec((FRAMES, 1, SUB, SIZE), lambda h, order_ref: (0, h, 0, 0)),
-                pl.BlockSpec(memory_space=pl.ANY),
-            ],
-            out_specs=pl.BlockSpec((1, POS, SIZE), lambda h, order_ref: (order_ref[SPAT + h], 0, 0)),
-        ),
+        in_specs=[smem, whole(), whole(pl.ANY)],
+        out_specs=whole(pl.ANY),
+        scratch_shapes=[pltpu.VMEM((TEMP, POS, SIZE), BF16), pltpu.SemaphoreType.DMA((TEMP,))],
         input_output_aliases={2: 0},
-        compiler_params=params(),
+        compiler_params=params(16),
         name="join",
     )(order, temporal_out, spatial)
     return jnp.transpose(out, (1, 0, 2))

time: 102 us -> 98.8 us (0.969); the launches traced: 100 us -> 98.2 us
  local copies, waits for them, and re-layouts: 3.14 us -> 0.85 us
    ppermute x6, waiting for transfers between devices: 6.15 us -> 3.48 us  [route(): return lax.ppermute(block, 'ctx', pairs)]
    unnamed x20 -> x14, local copies, waits for them, and re-layouts: 2.95 us -> 0.66 us
    all_to_all x2, waiting for transfers between devices: 18.2 us -> 20 us  [swap_all(): return lax.all_to_all(block, 'ctx', split_axis=0, concat_axis=0, tiled=True)]
    pallas_call x1, Pallas kernels: 1.73 us -> 3.21 us  [shards(): pl.pallas_call(norm_kernel, out_shape=(bf16(SPAT, POS, SIZE), bf16(2, SPA...]
    pallas_call x2, Pallas kernels: 6.05 us -> 4.99 us  [the longest x1 3.71 us: shards(): pl.pallas_call(spatial_kernel, out_shape=bf16(GROUP, POS, SIZE), in_specs...]
  transfers between devices with their start and end apart: 8 -> 8, of which waited for: 2 -> 3; matrix products, arithmetic and copies ran while one was open for 1% -> 1% of each run, Pallas kernels for 6% -> 5%
where the time goes in v2:
time: 98.8 us; the launch traced here: 98.2 us
  starting transfers between devices  51 us (52%)
  waiting for transfers between devices  23.5 us (24%)
  Pallas kernels  11.5 us (12%)
  blocking collectives  10.3 us (10%)
    all_to_all x2, starting transfers between devices, swap_all(): return lax.all_to_all(block, 'ctx', split_axis=0, concat_axis=0, tiled=True)  34.9 us
    all_to_all x2, waiting for transfers between devices, swap_all(): return lax.all_to_all(block, 'ctx', split_axis=0, concat_axis=0, tiled=True)  20 us
    ppermute x6, starting transfers between devices, route(): return lax.ppermute(block, 'ctx', pairs)  16.1 us
    psum x1, blocking collectives, shards(): sums = lax.psum(sums, 'head')  10.3 us
    pallas_call x1, Pallas kernels, shards(): pl.pallas_call(spatial_kernel, out_shape=bf16(GROUP, POS, SIZE), in_specs...  3.71 us
    ppermute x6, waiting for transfers between devices, route(): return lax.ppermute(block, 'ctx', pairs)  3.48 us
    pallas_call x1, Pallas kernels, shards(): pl.pallas_call(norm_kernel, out_shape=(bf16(SPAT, POS, SIZE), bf16(2, SPA...  3.21 us
  transfers between devices with their start and end apart: 8, of which 3 were waited for; matrix products, arithmetic and copies ran while one was open for 1% of the time, Pallas kernels for 5%

profile of v2, /device:TPU:1, one launch (start us, length us, event | category | flops | bytes accessed | tf_op | source)
XLA Modules:
  0.0 98.2 jit_solution(8514140867696039529)
XLA Ops:
  0.0 1.9 %sums.1 = f32[2,256]{1,0:T(2,128)} custom-call(bf16[5,256,128]{2,1,0:T(8,128)(2,1)} %bitcast.8, bf16[5,256,128]{2,1,0:T(8,128)(2,1)} %bitcast.10), custom_call_target="tpu_custom_call" | custom-call | tf_op jit(solution)/shard_map/sums/pallas_call | solution.py:216
  1.9 10.3 %psum.7.sums_ref = f32[2,256]{1,0:T(2,128)} all-reduce(f32[2,256]{1,0:T(2,128)} %sums.1), channel_id=1, replica_groups=mesh['ctx'=128,'head'=4] {'head'}, use_global_device_ids=true, to_apply=%region_2.3 | all-reduce | flops 512 | bytes 4096 | tf_op jit(solution)/shard_map/psum | solution.py:229
  12.2 3.2 %norm.1 = (bf16[3,256,128]{2,1,0:T(8,128)(2,1)}, bf16[2,3,256,128]{3,2,1,0:T(8,128)(2,1)}, bf16[128,6,2,128]{3,2,1,0:T(2,128)(2,1)}) custom-call(s32[5]{0:T(128)} %class_ref.1, f32[2,256]{1,0:T(2,128)} %psum.7.sums_ref, f32[5,128]{1,0:T(8,128)} %q_gain_ref.1, f32[5,128]{1,0:T(8,128)} %k_gain_ref.1, bf16[5,256,128]{2,1,0:T(8,128)(2,1)} %bitcast.9, ...), custom_call_target="tpu_custom_call" | custom-call | tf_op jit(solution)/shard_map/norm/pallas_call | solution.py:230
  15.4 21.7 %all-to-all-start = ((bf16[128,6,2,128]{3,2,1,0:T(2,128)(2,1)}), bf16[128,6,2,128]{3,2,1,0:T(2,128)(2,1)S(1)}, u32[]{:S(2)}, u32[]{:S(2)}) async-start(bf16[128,6,2,128]{3,2,1,0:T(2,128)(2,1)} %get-tuple-element.15), calls=%async_computation | async-start | bytes 786432 | tf_op jit(solution)/shard_map/all_to_all | solution.py:211
  37.2 2.8 %collective-permute-start.2 = (bf16[2,3,256,128]{3,2,1,0:T(8,128)(2,1)S(1)}, bf16[2,3,256,128]{3,2,1,0:T(8,128)(2,1)S(1)}, u32[]{:S(2)}, u32[]{:S(2)}) collective-permute-start(bf16[2,3,256,128]{3,2,1,0:T(8,128)(2,1)S(1)} %copy-done), channel_id=1, source_target_pairs={{0,4},{4,0},{8,12},{12,8},{16,20},{20,16},{24,28},{28,24},{32,36},... | collective-permute-start | bytes 1179656 | tf_op jit(solution)/shard_map/ppermute | solution.py:164
  40.0 1.3 %collective-permute-start.1 = (bf16[2,3,256,128]{3,2,1,0:T(8,128)(2,1)S(1)}, bf16[2,3,256,128]{3,2,1,0:T(8,128)(2,1)S(1)}, u32[]{:S(2)}, u32[]{:S(2)}) collective-permute-start(bf16[2,3,256,128]{3,2,1,0:T(8,128)(2,1)S(1)} %copy-done), channel_id=1, source_target_pairs={{8,0},{12,4},{16,8},{20,12},{24,16},{28,20},{32,24},{36,28},{40,32... | collective-permute-start | bytes 1179656 | tf_op jit(solution)/shard_map/ppermute | solution.py:164
  41.3 4.0 %collective-permute-start = (bf16[2,3,256,128]{3,2,1,0:T(8,128)(2,1)S(1)}, bf16[2,3,256,128]{3,2,1,0:T(8,128)(2,1)S(1)}, u32[]{:S(2)}, u32[]{:S(2)}) collective-permute-start(bf16[2,3,256,128]{3,2,1,0:T(8,128)(2,1)S(1)} %copy-done), channel_id=1, source_target_pairs={{0,8},{4,12},{8,16},{12,20},{16,24},{20,28},{24,32},{28,36},{32,40... | collective-permute-start | bytes 1179656 | tf_op jit(solution)/shard_map/ppermute | solution.py:164
  45.4 0.6 copy-done.5
  46.0 0.1 compare_convert_fusion
  46.1 0.6 multiply_reduce_fusion
  46.7 0.1 broadcast_in_dim.29
  46.7 0.1 reshape_reshape.3.bias_ref
  46.8 18.2 %all-to-all-done.x_ref = bf16[128,6,2,128]{3,2,1,0:T(2,128)(2,1)S(1)} async-done(((bf16[128,6,2,128]{3,2,1,0:T(2,128)(2,1)}), bf16[128,6,2,128]{3,2,1,0:T(2,128)(2,1)S(1)}, u32[]{:S(2)}, u32[]{:S(2)}) %all-to-all-start) | async-done | bytes 393248 | tf_op jit(solution)/shard_map/all_to_all | solution.py:211
  65.0 1.4 %temporal.1 = bf16[128,2,2,128]{3,2,1,0:T(2,128)(2,1)} custom-call(bf16[128,6,2,128]{3,2,1,0:T(2,128)(2,1)S(1)} %all-to-all-done.x_ref), custom_call_target="tpu_custom_call" | custom-call | tf_op jit(solution)/shard_map/temporal/pallas_call | solution.py:245
  66.4 13.1 %all-to-all-start.1 = ((bf16[128,2,2,128]{3,2,1,0:T(2,128)(2,1)}), bf16[128,2,2,128]{3,2,1,0:T(2,128)(2,1)S(1)}, u32[]{:S(2)}, u32[]{:S(2)}) async-start(bf16[128,2,2,128]{3,2,1,0:T(2,128)(2,1)} %temporal.1), calls=%async_computation.1 | async-start | bytes 262144 | tf_op jit(solution)/shard_map/all_to_all | solution.py:211
  79.6 3.7 %collective-permute-start.3 = (bf16[2,3,256,128]{3,2,1,0:T(8,128)(2,1)S(1)}, bf16[2,3,256,128]{3,2,1,0:T(8,128)(2,1)S(1)}, u32[]{:S(2)}, u32[]{:S(2)}) collective-permute-start(bf16[2,3,256,128]{3,2,1,0:T(8,128)(2,1)S(1)} %broadcast_select_fusion), channel_id=1, source_target_pairs={{4,8},{8,4},{12,16},{16,12},{20,24},{24,20},{28,32},{32,28},{36,40... | collective-permute-start | bytes 1179656 | tf_op jit(solution)/shard_map/ppermute | solution.py:164
  83.3 1.9 %collective-permute-start.4 = (bf16[2,3,256,128]{3,2,1,0:T(8,128)(2,1)S(1)}, bf16[2,3,256,128]{3,2,1,0:T(8,128)(2,1)S(1)}, u32[]{:S(2)}, u32[]{:S(2)}) collective-permute-start(bf16[2,3,256,128]{3,2,1,0:T(8,128)(2,1)S(1)} %collective-permute-done.refs_1_), channel_id=1, source_target_pairs={{0,4},{4,0},{8,12},{12,8},{16,20},{20,16},{24,28},{28,24},{32,36},... | collective-permute-start | bytes 1179656 | tf_op jit(solution)/shard_map/ppermute | solution.py:164
  85.2 2.4 %collective-permute-start.5 = (bf16[2,3,256,128]{3,2,1,0:T(8,128)(2,1)S(1)}, bf16[2,3,256,128]{3,2,1,0:T(8,128)(2,1)S(1)}, u32[]{:S(2)}, u32[]{:S(2)}) collective-permute-start(bf16[2,3,256,128]{3,2,1,0:T(8,128)(2,1)S(1)} %collective-permute-done.1.refs_5_), channel_id=1, source_target_pairs={{0,4},{4,0},{8,12},{12,8},{16,20},{20,16},{24,28},{28,24},{32,36},... | collective-permute-start | bytes 1179656 | tf_op jit(solution)/shard_map/ppermute | solution.py:164
  87.7 0.2 convert_reduce_fusion
  87.8 0.1 select_reduce_fusion.order_ref
  87.9 3.5 %collective-permute-done.3.refs_0_ = bf16[2,3,256,128]{3,2,1,0:T(8,128)(2,1)S(1)} collective-permute-done((bf16[2,3,256,128]{3,2,1,0:T(8,128)(2,1)S(1)}, bf16[2,3,256,128]{3,2,1,0:T(8,128)(2,1)S(1)}, u32[]{:S(2)}, u32[]{:S(2)}) %collective-permute-start.3) | collective-permute-done | bytes 393248 | tf_op jit(solution)/shard_map/ppermute | solution.py:164
  91.4 3.7 %spatial.1.spatial_ref = bf16[5,256,128]{2,1,0:T(8,128)(2,1)} custom-call(s32[5]{0:T(128)S(1)} %select_reduce_fusion.order_ref, f32[4,1792]{1,0:T(4,128)S(1)} %reshape_reshape.3.bias_ref, bf16[3,256,128]{2,1,0:T(8,128)(2,1)S(1)} %copy-done.1, bf16[2,3,256,128]{3,2,1,0:T(8,128)(2,1)S(1)} %collective-permute-done.3.refs_0_, ...), custom_call_target="tpu_custom_call" | custom-call | tf_op jit(solution)/shard_map/spatial/pallas_call | solution.py:260
  95.1 1.8 %all-to-all-done.1.moved_ref = bf16[128,2,2,128]{3,2,1,0:T(2,128)(2,1)S(1)} async-done(((bf16[128,2,2,128]{3,2,1,0:T(2,128)(2,1)}), bf16[128,2,2,128]{3,2,1,0:T(2,128)(2,1)S(1)}, u32[]{:S(2)}, u32[]{:S(2)}) %all-to-all-start.1) | async-done | bytes 131104 | tf_op jit(solution)/shard_map/all_to_all | solution.py:211
  97.0 1.3 %join.1 = bf16[5,256,128]{2,1,0:T(8,128)(2,1)} custom-call(s32[5]{0:T(128)S(1)} %select_reduce_fusion.order_ref, bf16[128,2,2,128]{3,2,1,0:T(2,128)(2,1)S(1)} %all-to-all-done.1.moved_ref, bf16[5,256,128]{2,1,0:T(8,128)(2,1)} %spatial.1.spatial_ref), custom_call_target="tpu_custom_call", output_to_operand_aliasing={{}: (2, {})} | custom-call | tf_op jit(solution)/shard_map/join/pallas_call | solution.py:273
  (23 shorter events, 0.2 us)
Async XLA Ops:
  15.4 21.7 %copy-start = (bf16[2,3,256,128]{3,2,1,0:T(8,128)(2,1)S(1)}, bf16[2,3,256,128]{3,2,1,0:T(8,128)(2,1)}, u32[]{:S(2)}) copy-start(bf16[2,3,256,128]{3,2,1,0:T(8,128)(2,1)} %get-tuple-element.16.refs_3_) | copy-start | bytes 1179652
  15.4 49.6 %all-to-all-start = ((bf16[128,6,2,128]{3,2,1,0:T(2,128)(2,1)}), bf16[128,6,2,128]{3,2,1,0:T(2,128)(2,1)S(1)}, u32[]{:S(2)}, u32[]{:S(2)}) async-start(bf16[128,6,2,128]{3,2,1,0:T(2,128)(2,1)} %get-tuple-element.15), calls=%async_computation | async-start | bytes 786432 | tf_op jit(solution)/shard_map/all_to_all | solution.py:211
  37.2 29.2 %collective-permute-start.2 = (bf16[2,3,256,128]{3,2,1,0:T(8,128)(2,1)S(1)}, bf16[2,3,256,128]{3,2,1,0:T(8,128)(2,1)S(1)}, u32[]{:S(2)}, u32[]{:S(2)}) collective-permute-start(bf16[2,3,256,128]{3,2,1,0:T(8,128)(2,1)S(1)} %copy-done), channel_id=1, source_target_pairs={{0,4},{4,0},{8,12},{12,8},{16,20},{20,16},{24,28},{28,24},{32,36},... | collective-permute-start | bytes 1179656 | tf_op jit(solution)/shard_map/ppermute | solution.py:164
  40.0 26.4 %collective-permute-start.1 = (bf16[2,3,256,128]{3,2,1,0:T(8,128)(2,1)S(1)}, bf16[2,3,256,128]{3,2,1,0:T(8,128)(2,1)S(1)}, u32[]{:S(2)}, u32[]{:S(2)}) collective-permute-start(bf16[2,3,256,128]{3,2,1,0:T(8,128)(2,1)S(1)} %copy-done), channel_id=1, source_target_pairs={{8,0},{12,4},{16,8},{20,12},{24,16},{28,20},{32,24},{36,28},{40,32... | collective-permute-start | bytes 1179656 | tf_op jit(solution)/shard_map/ppermute | solution.py:164
  41.3 25.1 %collective-permute-start = (bf16[2,3,256,128]{3,2,1,0:T(8,128)(2,1)S(1)}, bf16[2,3,256,128]{3,2,1,0:T(8,128)(2,1)S(1)}, u32[]{:S(2)}, u32[]{:S(2)}) collective-permute-start(bf16[2,3,256,128]{3,2,1,0:T(8,128)(2,1)S(1)} %copy-done), channel_id=1, source_target_pairs={{0,8},{4,12},{8,16},{12,20},{16,24},{20,28},{24,32},{28,36},{32,40... | collective-permute-start | bytes 1179656 | tf_op jit(solution)/shard_map/ppermute | solution.py:164
  45.3 0.7 copy-start.5
  45.3 0.7 copy-start.6
  45.3 0.7 copy-start.4
  45.3 0.7 copy-start.2
  66.4 30.5 %all-to-all-start.1 = ((bf16[128,2,2,128]{3,2,1,0:T(2,128)(2,1)}), bf16[128,2,2,128]{3,2,1,0:T(2,128)(2,1)S(1)}, u32[]{:S(2)}, u32[]{:S(2)}) async-start(bf16[128,2,2,128]{3,2,1,0:T(2,128)(2,1)} %temporal.1), calls=%async_computation.1 | async-start | bytes 262144 | tf_op jit(solution)/shard_map/all_to_all | solution.py:211
  79.5 8.1 %copy-start.3 = (s32[5]{0:T(128)S(1)}, s32[5]{0:T(128)}, u32[]{:S(2)}) copy-start(s32[5]{0:T(128)} %class_ref.1) | copy-start | bytes 64
  79.5 11.9 %copy-start.1 = (bf16[3,256,128]{2,1,0:T(8,128)(2,1)S(1)}, bf16[3,256,128]{2,1,0:T(8,128)(2,1)}, u32[]{:S(2)}) copy-start(bf16[3,256,128]{2,1,0:T(8,128)(2,1)} %get-tuple-element.18.q_ref) | copy-start | bytes 589828
  79.6 11.8 %collective-permute-start.3 = (bf16[2,3,256,128]{3,2,1,0:T(8,128)(2,1)S(1)}, bf16[2,3,256,128]{3,2,1,0:T(8,128)(2,1)S(1)}, u32[]{:S(2)}, u32[]{:S(2)}) collective-permute-start(bf16[2,3,256,128]{3,2,1,0:T(8,128)(2,1)S(1)} %broadcast_select_fusion), channel_id=1, source_target_pairs={{4,8},{8,4},{12,16},{16,12},{20,24},{24,20},{28,32},{32,28},{36,40... | collective-permute-start | bytes 1179656 | tf_op jit(solution)/shard_map/ppermute | solution.py:164
  83.3 8.1 %collective-permute-start.4 = (bf16[2,3,256,128]{3,2,1,0:T(8,128)(2,1)S(1)}, bf16[2,3,256,128]{3,2,1,0:T(8,128)(2,1)S(1)}, u32[]{:S(2)}, u32[]{:S(2)}) collective-permute-start(bf16[2,3,256,128]{3,2,1,0:T(8,128)(2,1)S(1)} %collective-permute-done.refs_1_), channel_id=1, source_target_pairs={{0,4},{4,0},{8,12},{12,8},{16,20},{20,16},{24,28},{28,24},{32,36},... | collective-permute-start | bytes 1179656 | tf_op jit(solution)/shard_map/ppermute | solution.py:164
  85.2 6.2 %collective-permute-start.5 = (bf16[2,3,256,128]{3,2,1,0:T(8,128)(2,1)S(1)}, bf16[2,3,256,128]{3,2,1,0:T(8,128)(2,1)S(1)}, u32[]{:S(2)}, u32[]{:S(2)}) collective-permute-start(bf16[2,3,256,128]{3,2,1,0:T(8,128)(2,1)S(1)} %collective-permute-done.1.refs_5_), channel_id=1, source_target_pairs={{0,4},{4,0},{8,12},{12,8},{16,20},{20,16},{24,28},{28,24},{32,36},... | collective-permute-start | bytes 1179656 | tf_op jit(solution)/shard_map/ppermute | solution.py:164

commit v3 on v2

--- a/solution.py
+++ b/solution.py
@@ -43,16 +43,20 @@
 
 
 def sums_kernel(q_ref, k_ref, sums_ref, q_buf, k_buf, sems):
+    half = POS // 2
     fetches = []
     for row, (x_ref, x_buf) in enumerate(((q_ref, q_buf), (k_ref, k_buf))):
         for head in range(GROUP):
-            fetch = pltpu.make_async_copy(x_ref.at[head], x_buf.at[head], sems.at[row * GROUP + head])
-            fetch.start()
-            fetches.append(fetch)
+            for part in range(2):
+                rows = pl.ds(part * half, half)
+                sem = sems.at[(row * GROUP + head) * 2 + part]
+                fetches.append(pltpu.make_async_copy(x_ref.at[head, rows], x_buf.at[head, rows], sem))
+                fetches[-1].start()
     for row, x_buf in enumerate((q_buf, k_buf)):
         total = jnp.zeros((POS, SIZE), F32)
         for head in range(GROUP):
-            fetches[row * GROUP + head].wait()
+            for part in range(2):
+                fetches[(row * GROUP + head) * 2 + part].wait()
             part = x_buf[head].astype(F32)
             total = total + part * part
         sums_ref[row : row + 1] = jnp.sum(total.T, axis=0, keepdims=True)
@@ -73,26 +77,37 @@
     return [jnp.broadcast_to(factors[row : row + 1], (SIZE, POS)).T for row in range(2)]
 
 
-def norm_kernel(
-    class_ref, sums_ref, q_gain_ref, k_gain_ref, q_ref, k_ref, v_ref, qs_ref, kvs_ref, chunk_ref, buf_ref, sems
-):
-    spat, temp = sorted_heads(class_ref)
-    heads = spat + temp
-    fetches = fetched((k_ref, v_ref, q_ref), heads, buf_ref, sems)
+def norm_temporal_kernel(class_ref, sums_ref, q_gain_ref, k_gain_ref, q_ref, k_ref, v_ref, chunk_ref, buf_ref, sems):
+    _, temp = sorted_heads(class_ref)
+    fetches = fetched((q_ref, k_ref, v_ref), temp, buf_ref, sems)
     factors = factors_of(sums_ref)
     for place, fetch in enumerate(fetches):
-        t, r = divmod(place, GROUP)
+        t, r = divmod(place, TEMP)
         fetch.wait()
         rows = buf_ref[place]
-        if t != 1:
-            gain = (k_gain_ref, None, q_gain_ref)[t][pl.ds(heads[r], 1)]
-            rows = (rows.astype(F32) * factors[1 - t // 2] * gain).astype(BF16)
-        if r >= SPAT:
-            chunk_ref[:, (1, 2, 0)[t] * TEMP + r - SPAT] = rows.reshape(FRAMES, SUB, SIZE)
-        elif t < 2:
-            kvs_ref[t, r] = rows
+        if t < 2:
+            gain = (q_gain_ref, k_gain_ref)[t][pl.ds(temp[r], 1)]
+            rows = (rows.astype(F32) * factors[t] * gain).astype(BF16)
+        chunk_ref[:, place] = rows.reshape(FRAMES, SUB, SIZE)
+
+
+def norm_spatial_kernel(
+    class_ref, sums_ref, q_gain_ref, k_gain_ref, q_ref, k_ref, v_ref, qs_ref, kvs_ref, buf_ref, sems
+):
+    spat, _ = sorted_heads(class_ref)
+    fetches = fetched((q_ref, k_ref, v_ref), spat, buf_ref, sems)
+    factors = factors_of(sums_ref)
+    for place, fetch in enumerate(fetches):
+        t, r = divmod(place, SPAT)
+        fetch.wait()
+        rows = buf_ref[place]
+        if t < 2:
+            gain = (q_gain_ref, k_gain_ref)[t][pl.ds(spat[r], 1)]
+            rows = (rows.astype(F32) * factors[t] * gain).astype(BF16)
+        if t == 0:
+            qs_ref[r] = rows
         else:
-            qs_ref[r] = rows
+            kvs_ref[t - 1, r] = rows
 
 
 def dot_t(a, b):
@@ -221,26 +236,33 @@
         scratch_shapes=[
             pltpu.VMEM((GROUP, POS, SIZE), BF16),
             pltpu.VMEM((GROUP, POS, SIZE), BF16),
-            pltpu.SemaphoreType.DMA((2 * GROUP,)),
+            pltpu.SemaphoreType.DMA((4 * GROUP,)),
         ],
         compiler_params=params(60),
         name="sums",
     )(q, k)
     sums = lax.psum(sums, "head")
-    q_own, kv_own, chunk = pl.pallas_call(
-        norm_kernel,
-        out_shape=(
-            bf16(SPAT, POS, SIZE),
-            bf16(2, SPAT, POS, SIZE),
-            bf16(FRAMES, 3 * TEMP, SUB, SIZE),
-        ),
-        in_specs=[whole(pltpu.SMEM)] + [whole()] * 3 + [whole(pl.ANY)] * 3,
-        out_specs=(whole(),) * 3,
-        scratch_shapes=[pltpu.VMEM((3 * GROUP, POS, SIZE), BF16), pltpu.SemaphoreType.DMA((3 * GROUP,))],
+    norm_specs = [whole(pltpu.SMEM)] + [whole()] * 3 + [whole(pl.ANY)] * 3
+    chunk = pl.pallas_call(
+        norm_temporal_kernel,
+        out_shape=bf16(FRAMES, 3 * TEMP, SUB, SIZE),
+        in_specs=norm_specs,
+        out_specs=whole(),
+        scratch_shapes=[pltpu.VMEM((3 * TEMP, POS, SIZE), BF16), pltpu.SemaphoreType.DMA((3 * TEMP,))],
         compiler_params=params(60),
-        name="norm",
+        name="norm_temporal",
     )(head_class, sums, query_gain, key_gain, q, k, v)
+    chunk, sums = lax.optimization_barrier((chunk, sums))
     rows = swap_all(chunk)
+    q_own, kv_own = pl.pallas_call(
+        norm_spatial_kernel,
+        out_shape=(bf16(SPAT, POS, SIZE), bf16(2, SPAT, POS, SIZE)),
+        in_specs=norm_specs,
+        out_specs=(whole(),) * 2,
+        scratch_shapes=[pltpu.VMEM((3 * SPAT, POS, SIZE), BF16), pltpu.SemaphoreType.DMA((3 * SPAT,))],
+        compiler_params=params(16),
+        name="norm_spatial",
+    )(head_class, sums, query_gain, key_gain, q, k, v)
     first = first_window(kv_own)
     outputs = pl.pallas_call(
         temporal_kernel,

time: 98.8 us -> 98.5 us (level)
  waiting for transfers between devices: 23.5 us -> 21.9 us
  Pallas kernels: 11.5 us -> 12.8 us
    all_to_all x2, waiting for transfers between devices: 20 us -> 18.3 us  [swap_all(): return lax.all_to_all(block, 'ctx', split_axis=0, concat_axis=0, tiled=True)]
    pallas_call x1 -> x2, Pallas kernels: 3.21 us -> 4.44 us  [the longest x1 2.76 us: shards(): pl.pallas_call(norm_temporal_kernel, out_shape=bf16(FRAMES, 3 * TEMP, SUB...]
  transfers between devices with their start and end apart: 8 -> 8, of which waited for: 3 -> 3; matrix products, arithmetic and copies ran while one was open for 1% -> 1% of each run, Pallas kernels for 5% -> 7%
where the time goes in v3:
time: 98.5 us; the launch traced here: 97.9 us
  starting transfers between devices  50.8 us (52%)
  waiting for transfers between devices  21.9 us (22%)
  Pallas kernels  12.8 us (13%)
  blocking collectives  10.3 us (10%)
    all_to_all x2, starting transfers between devices, swap_all(): return lax.all_to_all(block, 'ctx', split_axis=0, concat_axis=0, tiled=True)  34.9 us
    all_to_all x2, waiting for transfers between devices, swap_all(): return lax.all_to_all(block, 'ctx', split_axis=0, concat_axis=0, tiled=True)  18.3 us
    ppermute x6, starting transfers between devices, route(): return lax.ppermute(block, 'ctx', pairs)  16 us
    psum x1, blocking collectives, shards(): sums = lax.psum(sums, 'head')  10.3 us
    pallas_call x1, Pallas kernels, shards(): pl.pallas_call(spatial_kernel, out_shape=bf16(GROUP, POS, SIZE), in_specs...  3.74 us
    ppermute x6, waiting for transfers between devices, route(): return lax.ppermute(block, 'ctx', pairs)  3.64 us
    pallas_call x1, Pallas kernels, shards(): pl.pallas_call(norm_temporal_kernel, out_shape=bf16(FRAMES, 3 * TEMP, SUB...  2.76 us
  transfers between devices with their start and end apart: 8, of which 3 were waited for; matrix products, arithmetic and copies ran while one was open for 1% of the time, Pallas kernels for 7%

profile of v3, /device:TPU:1, one launch (start us, length us, event | category | flops | bytes accessed | tf_op | source)
XLA Modules:
  0.0 97.9 jit_solution(16101813976695419222)
XLA Ops:
  0.0 1.9 %sums.1 = f32[2,256]{1,0:T(2,128)} custom-call(bf16[5,256,128]{2,1,0:T(8,128)(2,1)} %bitcast.8, bf16[5,256,128]{2,1,0:T(8,128)(2,1)} %bitcast.11), custom_call_target="tpu_custom_call" | custom-call | tf_op jit(solution)/shard_map/sums/pallas_call | solution.py:231
  1.9 10.3 %psum.7.sums_ref = f32[2,256]{1,0:T(2,128)} all-reduce(f32[2,256]{1,0:T(2,128)} %sums.1), channel_id=1, replica_groups=mesh['ctx'=128,'head'=4] {'head'}, use_global_device_ids=true, to_apply=%region_2.3 | all-reduce | flops 512 | bytes 4096 | tf_op jit(solution)/shard_map/psum | solution.py:244
  12.2 2.8 %norm_temporal.1 = bf16[128,6,2,128]{3,2,1,0:T(2,128)(2,1)} custom-call(s32[5]{0:T(128)} %class_ref.3, f32[2,256]{1,0:T(2,128)} %psum.7.sums_ref, f32[5,128]{1,0:T(8,128)} %q_gain_ref.3, f32[5,128]{1,0:T(8,128)} %k_gain_ref.3, bf16[5,256,128]{2,1,0:T(8,128)(2,1)} %bitcast.9, bf16[5,256,128]{2,1,0:T(8,128)(2,1)} %bitcast.12, bf16[5,256,128]{2,1,0:T(8,128)(2,1)} %bitcast.14), custom_call_target="tpu_custom_call" | custom-call | tf_op jit(solution)/shard_map/norm_temporal/pallas_call | solution.py:246
  15.1 21.7 %all-to-all-start = ((bf16[128,6,2,128]{3,2,1,0:T(2,128)(2,1)}), bf16[128,6,2,128]{3,2,1,0:T(2,128)(2,1)S(1)}, u32[]{:S(2)}, u32[]{:S(2)}) async-start(bf16[128,6,2,128]{3,2,1,0:T(2,128)(2,1)} %norm_temporal.1), calls=%async_computation | async-start | bytes 786432 | tf_op jit(solution)/shard_map/all_to_all | solution.py:226
  36.9 1.7 %norm_spatial.1 = (bf16[3,256,128]{2,1,0:T(8,128)(2,1)S(1)}, bf16[2,3,256,128]{3,2,1,0:T(8,128)(2,1)S(1)}) custom-call(s32[5]{0:T(128)S(1)} %copy-done.6, f32[2,256]{1,0:T(2,128)S(1)} %copy-done.3, f32[5,128]{1,0:T(8,128)S(1)} %copy-done.4, f32[5,128]{1,0:T(8,128)S(1)} %copy-done.5, bf16[5,256,128]{2,1,0:T(8,128)(2,1)S(1)} %bitcast.10, ...), custom_call_target="tpu_custom_call" | custom-call | tf_op jit(solution)/shard_map/norm_spatial/pallas_call | solution.py:257
  38.6 2.8 %collective-permute-start.2 = (bf16[2,3,256,128]{3,2,1,0:T(8,128)(2,1)S(1)}, bf16[2,3,256,128]{3,2,1,0:T(8,128)(2,1)S(1)}, u32[]{:S(2)}, u32[]{:S(2)}) collective-permute-start(bf16[2,3,256,128]{3,2,1,0:T(8,128)(2,1)S(1)} %get-tuple-element.18.refs_3_), channel_id=1, source_target_pairs={{0,4},{4,0},{8,12},{12,8},{16,20},{20,16},{24,28},{28,24},{32,36},... | collective-permute-start | bytes 1179656 | tf_op jit(solution)/shard_map/ppermute | solution.py:179
  41.4 1.3 %collective-permute-start.1 = (bf16[2,3,256,128]{3,2,1,0:T(8,128)(2,1)S(1)}, bf16[2,3,256,128]{3,2,1,0:T(8,128)(2,1)S(1)}, u32[]{:S(2)}, u32[]{:S(2)}) collective-permute-start(bf16[2,3,256,128]{3,2,1,0:T(8,128)(2,1)S(1)} %get-tuple-element.18.refs_3_), channel_id=1, source_target_pairs={{8,0},{12,4},{16,8},{20,12},{24,16},{28,20},{32,24},{36,28},{40,32... | collective-permute-start | bytes 1179656 | tf_op jit(solution)/shard_map/ppermute | solution.py:179
  42.7 4.0 %collective-permute-start = (bf16[2,3,256,128]{3,2,1,0:T(8,128)(2,1)S(1)}, bf16[2,3,256,128]{3,2,1,0:T(8,128)(2,1)S(1)}, u32[]{:S(2)}, u32[]{:S(2)}) collective-permute-start(bf16[2,3,256,128]{3,2,1,0:T(8,128)(2,1)S(1)} %get-tuple-element.18.refs_3_), channel_id=1, source_target_pairs={{0,8},{4,12},{8,16},{12,20},{16,24},{20,28},{24,32},{28,36},{32,40... | collective-permute-start | bytes 1179656 | tf_op jit(solution)/shard_map/ppermute | solution.py:179
  46.9 0.6 copy-done.7
  47.4 0.6 multiply_reduce_fusion
  48.0 0.1 broadcast_in_dim.29
  48.1 0.1 reshape_reshape.3.bias_ref
  48.2 16.5 %all-to-all-done.x_ref = bf16[128,6,2,128]{3,2,1,0:T(2,128)(2,1)S(1)} async-done(((bf16[128,6,2,128]{3,2,1,0:T(2,128)(2,1)}), bf16[128,6,2,128]{3,2,1,0:T(2,128)(2,1)S(1)}, u32[]{:S(2)}, u32[]{:S(2)}) %all-to-all-start) | async-done | bytes 393248 | tf_op jit(solution)/shard_map/all_to_all | solution.py:226
  64.7 1.4 %temporal.1 = bf16[128,2,2,128]{3,2,1,0:T(2,128)(2,1)} custom-call(bf16[128,6,2,128]{3,2,1,0:T(2,128)(2,1)S(1)} %all-to-all-done.x_ref), custom_call_target="tpu_custom_call" | custom-call | tf_op jit(solution)/shard_map/temporal/pallas_call | solution.py:267
  66.0 13.1 %all-to-all-start.1 = ((bf16[128,2,2,128]{3,2,1,0:T(2,128)(2,1)}), bf16[128,2,2,128]{3,2,1,0:T(2,128)(2,1)S(1)}, u32[]{:S(2)}, u32[]{:S(2)}) async-start(bf16[128,2,2,128]{3,2,1,0:T(2,128)(2,1)} %temporal.1), calls=%async_computation.1 | async-start | bytes 262144 | tf_op jit(solution)/shard_map/all_to_all | solution.py:226
  79.2 3.5 %collective-permute-start.3 = (bf16[2,3,256,128]{3,2,1,0:T(8,128)(2,1)S(1)}, bf16[2,3,256,128]{3,2,1,0:T(8,128)(2,1)S(1)}, u32[]{:S(2)}, u32[]{:S(2)}) collective-permute-start(bf16[2,3,256,128]{3,2,1,0:T(8,128)(2,1)S(1)} %broadcast_select_fusion), channel_id=1, source_target_pairs={{4,8},{8,4},{12,16},{16,12},{20,24},{24,20},{28,32},{32,28},{36,40... | collective-permute-start | bytes 1179656 | tf_op jit(solution)/shard_map/ppermute | solution.py:179
  82.8 1.9 %collective-permute-start.4 = (bf16[2,3,256,128]{3,2,1,0:T(8,128)(2,1)S(1)}, bf16[2,3,256,128]{3,2,1,0:T(8,128)(2,1)S(1)}, u32[]{:S(2)}, u32[]{:S(2)}) collective-permute-start(bf16[2,3,256,128]{3,2,1,0:T(8,128)(2,1)S(1)} %collective-permute-done.refs_1_), channel_id=1, source_target_pairs={{0,4},{4,0},{8,12},{12,8},{16,20},{20,16},{24,28},{28,24},{32,36},... | collective-permute-start | bytes 1179656 | tf_op jit(solution)/shard_map/ppermute | solution.py:179
  84.7 2.4 %collective-permute-start.5 = (bf16[2,3,256,128]{3,2,1,0:T(8,128)(2,1)S(1)}, bf16[2,3,256,128]{3,2,1,0:T(8,128)(2,1)S(1)}, u32[]{:S(2)}, u32[]{:S(2)}) collective-permute-start(bf16[2,3,256,128]{3,2,1,0:T(8,128)(2,1)S(1)} %collective-permute-done.1.refs_5_), channel_id=1, source_target_pairs={{0,4},{4,0},{8,12},{12,8},{16,20},{20,16},{24,28},{28,24},{32,36},... | collective-permute-start | bytes 1179656 | tf_op jit(solution)/shard_map/ppermute | solution.py:179
  87.1 0.2 convert_reduce_fusion
  87.3 0.1 select_reduce_fusion.order_ref
  87.4 3.6 %collective-permute-done.3.refs_0_ = bf16[2,3,256,128]{3,2,1,0:T(8,128)(2,1)S(1)} collective-permute-done((bf16[2,3,256,128]{3,2,1,0:T(8,128)(2,1)S(1)}, bf16[2,3,256,128]{3,2,1,0:T(8,128)(2,1)S(1)}, u32[]{:S(2)}, u32[]{:S(2)}) %collective-permute-start.3) | collective-permute-done | bytes 393248 | tf_op jit(solution)/shard_map/ppermute | solution.py:179
  91.0 3.7 %spatial.1.spatial_ref = bf16[5,256,128]{2,1,0:T(8,128)(2,1)} custom-call(s32[5]{0:T(128)S(1)} %select_reduce_fusion.order_ref, f32[4,1792]{1,0:T(4,128)S(1)} %reshape_reshape.3.bias_ref, bf16[3,256,128]{2,1,0:T(8,128)(2,1)S(1)} %get-tuple-element.20.q_ref, bf16[2,3,256,128]{3,2,1,0:T(8,128)(2,1)S(1)} %collective-permute-done.3.refs_0_, ...), custom_call_target="tpu_custom_call" | custom-call | tf_op jit(solution)/shard_map/spatial/pallas_call | solution.py:282
  94.8 1.8 %all-to-all-done.1.moved_ref = bf16[128,2,2,128]{3,2,1,0:T(2,128)(2,1)S(1)} async-done(((bf16[128,2,2,128]{3,2,1,0:T(2,128)(2,1)}), bf16[128,2,2,128]{3,2,1,0:T(2,128)(2,1)S(1)}, u32[]{:S(2)}, u32[]{:S(2)}) %all-to-all-start.1) | async-done | bytes 131104 | tf_op jit(solution)/shard_map/all_to_all | solution.py:226
  96.6 1.3 %join.1 = bf16[5,256,128]{2,1,0:T(8,128)(2,1)} custom-call(s32[5]{0:T(128)S(1)} %select_reduce_fusion.order_ref, bf16[128,2,2,128]{3,2,1,0:T(2,128)(2,1)S(1)} %all-to-all-done.1.moved_ref, bf16[5,256,128]{2,1,0:T(8,128)(2,1)} %spatial.1.spatial_ref), custom_call_target="tpu_custom_call", output_to_operand_aliasing={{}: (2, {})} | custom-call | tf_op jit(solution)/shard_map/join/pallas_call | solution.py:295
  (32 shorter events, 0.2 us)
Async XLA Ops:
  12.2 24.6 %copy-start.2 = (bf16[256,5,128]{2,0,1:T(8,128)(2,1)S(1)}, bf16[256,5,128]{2,0,1:T(8,128)(2,1)}, u32[]{:S(2)}) copy-start(bf16[256,5,128]{2,0,1:T(8,128)(2,1)} %param.12) | copy-start | bytes 983044
  15.0 21.8 %copy-start = (bf16[256,5,128]{2,0,1:T(8,128)(2,1)S(1)}, bf16[256,5,128]{2,0,1:T(8,128)(2,1)}, u32[]{:S(2)}) copy-start(bf16[256,5,128]{2,0,1:T(8,128)(2,1)} %param.10) | copy-start | bytes 983044
  15.0 21.8 %copy-start.1 = (bf16[256,5,128]{2,0,1:T(8,128)(2,1)S(1)}, bf16[256,5,128]{2,0,1:T(8,128)(2,1)}, u32[]{:S(2)}) copy-start(bf16[256,5,128]{2,0,1:T(8,128)(2,1)} %param.11) | copy-start | bytes 983044
  15.0 21.8 %copy-start.3 = (f32[2,256]{1,0:T(2,128)S(1)}, f32[2,256]{1,0:T(2,128)}, u32[]{:S(2)}) copy-start(f32[2,256]{1,0:T(2,128)} %psum.7.sums_ref) | copy-start | bytes 6148
  15.0 21.8 %copy-start.4 = (f32[5,128]{1,0:T(8,128)S(1)}, f32[5,128]{1,0:T(8,128)}, u32[]{:S(2)}) copy-start(f32[5,128]{1,0:T(8,128)} %q_gain_ref.3) | copy-start | bytes 7684
  15.0 21.8 %copy-start.5 = (f32[5,128]{1,0:T(8,128)S(1)}, f32[5,128]{1,0:T(8,128)}, u32[]{:S(2)}) copy-start(f32[5,128]{1,0:T(8,128)} %k_gain_ref.3) | copy-start | bytes 7684
  15.0 21.8 %copy-start.6 = (s32[5]{0:T(128)S(1)}, s32[5]{0:T(128)}, u32[]{:S(2)}) copy-start(s32[5]{0:T(128)} %class_ref.3) | copy-start | bytes 64
  15.1 49.6 %all-to-all-start = ((bf16[128,6,2,128]{3,2,1,0:T(2,128)(2,1)}), bf16[128,6,2,128]{3,2,1,0:T(2,128)(2,1)S(1)}, u32[]{:S(2)}, u32[]{:S(2)}) async-start(bf16[128,6,2,128]{3,2,1,0:T(2,128)(2,1)} %norm_temporal.1), calls=%async_computation | async-start | bytes 786432 | tf_op jit(solution)/shard_map/all_to_all | solution.py:226
  36.9 9.9 %copy-start.9 = (s32[7]{0:T(128)S(1)}, s32[7]{0:T(128)}, u32[]{:S(2)}) copy-start(s32[7]{0:T(128)} %constant.36.clone) | copy-start | bytes 88
  36.9 9.9 %copy-start.10 = (s32[7]{0:T(128)S(1)}, s32[7]{0:T(128)}, u32[]{:S(2)}) copy-start(s32[7]{0:T(128)} %constant.35.clone) | copy-start | bytes 88
  36.9 9.9 %copy-start.8 = (s32[1,7]{1,0:T(1,128)S(1)}, s32[1,7]{1,0:T(1,128)}, u32[]{:S(2)}) copy-start(s32[1,7]{1,0:T(1,128)} %param.16) | copy-start | bytes 88
  38.6 27.4 %collective-permute-start.2 = (bf16[2,3,256,128]{3,2,1,0:T(8,128)(2,1)S(1)}, bf16[2,3,256,128]{3,2,1,0:T(8,128)(2,1)S(1)}, u32[]{:S(2)}, u32[]{:S(2)}) collective-permute-start(bf16[2,3,256,128]{3,2,1,0:T(8,128)(2,1)S(1)} %get-tuple-element.18.refs_3_), channel_id=1, source_target_pairs={{0,4},{4,0},{8,12},{12,8},{16,20},{20,16},{24,28},{28,24},{32,36},... | collective-permute-start | bytes 1179656 | tf_op jit(solution)/shard_map/ppermute | solution.py:179
  41.4 24.6 %collective-permute-start.1 = (bf16[2,3,256,128]{3,2,1,0:T(8,128)(2,1)S(1)}, bf16[2,3,256,128]{3,2,1,0:T(8,128)(2,1)S(1)}, u32[]{:S(2)}, u32[]{:S(2)}) collective-permute-start(bf16[2,3,256,128]{3,2,1,0:T(8,128)(2,1)S(1)} %get-tuple-element.18.refs_3_), channel_id=1, source_target_pairs={{8,0},{12,4},{16,8},{20,12},{24,16},{28,20},{32,24},{36,28},{40,32... | collective-permute-start | bytes 1179656 | tf_op jit(solution)/shard_map/ppermute | solution.py:179
  42.7 23.3 %collective-permute-start = (bf16[2,3,256,128]{3,2,1,0:T(8,128)(2,1)S(1)}, bf16[2,3,256,128]{3,2,1,0:T(8,128)(2,1)S(1)}, u32[]{:S(2)}, u32[]{:S(2)}) collective-permute-start(bf16[2,3,256,128]{3,2,1,0:T(8,128)(2,1)S(1)} %get-tuple-element.18.refs_3_), channel_id=1, source_target_pairs={{0,8},{4,12},{8,16},{12,20},{16,24},{20,28},{24,32},{28,36},{32,40... | collective-permute-start | bytes 1179656 | tf_op jit(solution)/shard_map/ppermute | solution.py:179
  46.7 0.7 copy-start.7
  66.0 30.6 %all-to-all-start.1 = ((bf16[128,2,2,128]{3,2,1,0:T(2,128)(2,1)}), bf16[128,2,2,128]{3,2,1,0:T(2,128)(2,1)S(1)}, u32[]{:S(2)}, u32[]{:S(2)}) async-start(bf16[128,2,2,128]{3,2,1,0:T(2,128)(2,1)} %temporal.1), calls=%async_computation.1 | async-start | bytes 262144 | tf_op jit(solution)/shard_map/all_to_all | solution.py:226
  79.2 11.8 %collective-permute-start.3 = (bf16[2,3,256,128]{3,2,1,0:T(8,128)(2,1)S(1)}, bf16[2,3,256,128]{3,2,1,0:T(8,128)(2,1)S(1)}, u32[]{:S(2)}, u32[]{:S(2)}) collective-permute-start(bf16[2,3,256,128]{3,2,1,0:T(8,128)(2,1)S(1)} %broadcast_select_fusion), channel_id=1, source_target_pairs={{4,8},{8,4},{12,16},{16,12},{20,24},{24,20},{28,32},{32,28},{36,40... | collective-permute-start | bytes 1179656 | tf_op jit(solution)/shard_map/ppermute | solution.py:179
  82.8 8.3 %collective-permute-start.4 = (bf16[2,3,256,128]{3,2,1,0:T(8,128)(2,1)S(1)}, bf16[2,3,256,128]{3,2,1,0:T(8,128)(2,1)S(1)}, u32[]{:S(2)}, u32[]{:S(2)}) collective-permute-start(bf16[2,3,256,128]{3,2,1,0:T(8,128)(2,1)S(1)} %collective-permute-done.refs_1_), channel_id=1, source_target_pairs={{0,4},{4,0},{8,12},{12,8},{16,20},{20,16},{24,28},{28,24},{32,36},... | collective-permute-start | bytes 1179656 | tf_op jit(solution)/shard_map/ppermute | solution.py:179
  84.7 6.3 %collective-permute-start.5 = (bf16[2,3,256,128]{3,2,1,0:T(8,128)(2,1)S(1)}, bf16[2,3,256,128]{3,2,1,0:T(8,128)(2,1)S(1)}, u32[]{:S(2)}, u32[]{:S(2)}) collective-permute-start(bf16[2,3,256,128]{3,2,1,0:T(8,128)(2,1)S(1)} %collective-permute-done.1.refs_5_), channel_id=1, source_target_pairs={{0,4},{4,0},{8,12},{12,8},{16,20},{20,16},{24,28},{28,24},{32,36},... | collective-permute-start | bytes 1179656 | tf_op jit(solution)/shard_map/ppermute | solution.py:179

commit v4 on v3

--- a/solution.py
+++ b/solution.py
@@ -77,18 +77,37 @@
     return [jnp.broadcast_to(factors[row : row + 1], (SIZE, POS)).T for row in range(2)]
 
 
-def norm_temporal_kernel(class_ref, sums_ref, q_gain_ref, k_gain_ref, q_ref, k_ref, v_ref, chunk_ref, buf_ref, sems):
+def norm_temporal_kernel(
+    class_ref, sums_hbm, q_gain_hbm, k_gain_hbm, q_ref, k_ref, v_ref, out_ref,
+    sums_ref, q_gain_ref, k_gain_ref, buf_ref, chunk_ref, sems, small_sems, out_sems
+):
+    small = []
+    for i, (src, dst) in enumerate(
+        ((sums_hbm, sums_ref), (q_gain_hbm, q_gain_ref), (k_gain_hbm, k_gain_ref))
+    ):
+        small.append(pltpu.make_async_copy(src, dst, small_sems.at[i]))
+        small[-1].start()
     _, temp = sorted_heads(class_ref)
     fetches = fetched((q_ref, k_ref, v_ref), temp, buf_ref, sems)
+    for copy in small:
+        copy.wait()
     factors = factors_of(sums_ref)
-    for place, fetch in enumerate(fetches):
-        t, r = divmod(place, TEMP)
-        fetch.wait()
-        rows = buf_ref[place]
-        if t < 2:
-            gain = (q_gain_ref, k_gain_ref)[t][pl.ds(temp[r], 1)]
-            rows = (rows.astype(F32) * factors[t] * gain).astype(BF16)
-        chunk_ref[:, place] = rows.reshape(FRAMES, SUB, SIZE)
+    sends = []
+    for t in (2, 0, 1):
+        for r in range(TEMP):
+            place = t * TEMP + r
+            fetches[place].wait()
+            rows = buf_ref[place]
+            if t < 2:
+                gain = (q_gain_ref, k_gain_ref)[t][pl.ds(temp[r], 1)]
+                rows = (rows.astype(F32) * factors[t] * gain).astype(BF16)
+            chunk_ref[t, :, r] = rows.reshape(FRAMES, SUB, SIZE)
+        sends.append(
+            pltpu.make_async_copy(chunk_ref.at[t], out_ref.at[:, pl.ds(t * TEMP, TEMP)], out_sems.at[t])
+        )
+        sends[-1].start()
+    for send in sends:
+        send.wait()
 
 
 def norm_spatial_kernel(
@@ -131,7 +150,8 @@
     return (out / jnp.sum(total, axis=1, keepdims=True)).astype(BF16)
 
 
-def temporal_kernel(x_ref, y_ref):
+def temporal_kernel(x_ref, out_ref, y_ref, sems):
+    sends = []
     query_row = lax.broadcasted_iota(jnp.int32, (POS, POS), 0) % SUB
     key_row = lax.broadcasted_iota(jnp.int32, (POS, POS), 1) % SUB
     bias = jnp.where(query_row == key_row, 0.0, UNSEEN)
@@ -141,7 +161,11 @@
         expo = jnp.exp2(scores - jnp.max(scores, axis=1, keepdims=True))
         total = jnp.sum(expo, axis=1, keepdims=True)
         out = jnp.dot(expo.astype(BF16), v, preferred_element_type=F32) / total
-        y_ref[:, head] = out.astype(BF16).reshape(FRAMES, SUB, SIZE)
+        y_ref[head, :, 0] = out.astype(BF16).reshape(FRAMES, SUB, SIZE)
+        sends.append(pltpu.make_async_copy(y_ref.at[head], out_ref.at[:, pl.ds(head, 1)], sems.at[head]))
+        sends[-1].start()
+    for send in sends:
+        send.wait()
 
 
 def spatial_kernel(order_ref, bias_ref, q_ref, *refs):
@@ -246,9 +270,18 @@
     chunk = pl.pallas_call(
         norm_temporal_kernel,
         out_shape=bf16(FRAMES, 3 * TEMP, SUB, SIZE),
-        in_specs=norm_specs,
-        out_specs=whole(),
-        scratch_shapes=[pltpu.VMEM((3 * TEMP, POS, SIZE), BF16), pltpu.SemaphoreType.DMA((3 * TEMP,))],
+        in_specs=[whole(pltpu.SMEM)] + [whole(pl.ANY)] * 6,
+        out_specs=whole(pl.ANY),
+        scratch_shapes=[
+            pltpu.VMEM((2, POS), F32),
+            pltpu.VMEM((GROUP, SIZE), F32),
+            pltpu.VMEM((GROUP, SIZE), F32),
+            pltpu.VMEM((3 * TEMP, POS, SIZE), BF16),
+            pltpu.VMEM((3, FRAMES, TEMP, SUB, SIZE), BF16),
+            pltpu.SemaphoreType.DMA((3 * TEMP,)),
+            pltpu.SemaphoreType.DMA((3,)),
+            pltpu.SemaphoreType.DMA((3,)),
+        ],
         compiler_params=params(60),
         name="norm_temporal",
     )(head_class, sums, query_gain, key_gain, q, k, v)
@@ -268,7 +301,11 @@
         temporal_kernel,
         out_shape=bf16(FRAMES, TEMP, SUB, SIZE),
         in_specs=[whole()],
-        out_specs=whole(),
+        out_specs=whole(pl.ANY),
+        scratch_shapes=[
+            pltpu.VMEM((TEMP, FRAMES, 1, SUB, SIZE), BF16),
+            pltpu.SemaphoreType.DMA((TEMP,)),
+        ],
         compiler_params=params(16),
         name="temporal",
     )(rows)

time: 98.5 us -> 98.6 us (level)
  no operation moved by 1% of the time
where the time goes in v4:
time: 98.6 us; the launch traced here: 98 us
  starting transfers between devices  50.8 us (52%)
  waiting for transfers between devices  21.9 us (22%)
  Pallas kernels  12.9 us (13%)
  blocking collectives  10.3 us (10%)
    all_to_all x2, starting transfers between devices, swap_all(): return lax.all_to_all(block, 'ctx', split_axis=0, concat_axis=0, tiled=True)  34.8 us
    all_to_all x2, waiting for transfers between devices, swap_all(): return lax.all_to_all(block, 'ctx', split_axis=0, concat_axis=0, tiled=True)  18.3 us
    ppermute x6, starting transfers between devices, route(): return lax.ppermute(block, 'ctx', pairs)  16 us
    psum x1, blocking collectives, shards(): sums = lax.psum(sums, 'head')  10.3 us
    pallas_call x1, Pallas kernels, shards(): pl.pallas_call(spatial_kernel, out_shape=bf16(GROUP, POS, SIZE), in_specs...  3.74 us
    ppermute x6, waiting for transfers between devices, route(): return lax.ppermute(block, 'ctx', pairs)  3.64 us
    pallas_call x1, Pallas kernels, shards(): pl.pallas_call(norm_temporal_kernel, out_shape=bf16(FRAMES, 3 * TEMP, SUB...  2.89 us
  transfers between devices with their start and end apart: 8, of which 3 were waited for; matrix products, arithmetic and copies ran while one was open for 1% of the time, Pallas kernels for 7%

profile of v4, /device:TPU:1, one launch (start us, length us, event | category | flops | bytes accessed | tf_op | source)
XLA Modules:
  0.0 98.0 jit_solution(3326866825375039437)
XLA Ops:
  0.0 1.9 %sums.1 = f32[2,256]{1,0:T(2,128)} custom-call(bf16[5,256,128]{2,1,0:T(8,128)(2,1)} %bitcast.8, bf16[5,256,128]{2,1,0:T(8,128)(2,1)} %bitcast.11), custom_call_target="tpu_custom_call" | custom-call | tf_op jit(solution)/shard_map/sums/pallas_call | solution.py:255
  1.9 10.3 %psum.7.sums_hbm.sums_ref = f32[2,256]{1,0:T(2,128)} all-reduce(f32[2,256]{1,0:T(2,128)} %sums.1), channel_id=1, replica_groups=mesh['ctx'=128,'head'=4] {'head'}, use_global_device_ids=true, to_apply=%region_2.3 | all-reduce | flops 512 | bytes 4096 | tf_op jit(solution)/shard_map/psum | solution.py:268
  12.2 2.9 %norm_temporal.1 = bf16[128,6,2,128]{3,2,1,0:T(2,128)(2,1)} custom-call(s32[5]{0:T(128)} %class_ref.3, f32[2,256]{1,0:T(2,128)} %psum.7.sums_hbm.sums_ref, f32[5,128]{1,0:T(8,128)} %q_gain_ref.1, f32[5,128]{1,0:T(8,128)} %k_gain_ref.1, bf16[5,256,128]{2,1,0:T(8,128)(2,1)} %bitcast.9, bf16[5,256,128]{2,1,0:T(8,128)(2,1)} %bitcast.12, ...), custom_call_target="tpu_custom_call" | custom-call | tf_op jit(solution)/shard_map/norm_temporal/pallas_call | solution.py:270
  15.2 21.7 %all-to-all-start = ((bf16[128,6,2,128]{3,2,1,0:T(2,128)(2,1)}), bf16[128,6,2,128]{3,2,1,0:T(2,128)(2,1)S(1)}, u32[]{:S(2)}, u32[]{:S(2)}) async-start(bf16[128,6,2,128]{3,2,1,0:T(2,128)(2,1)} %norm_temporal.1), calls=%async_computation | async-start | bytes 786432 | tf_op jit(solution)/shard_map/all_to_all | solution.py:250
  37.0 1.7 %norm_spatial.1 = (bf16[3,256,128]{2,1,0:T(8,128)(2,1)S(1)}, bf16[2,3,256,128]{3,2,1,0:T(8,128)(2,1)S(1)}) custom-call(s32[5]{0:T(128)S(1)} %copy-done.6, f32[2,256]{1,0:T(2,128)S(1)} %copy-done.3, f32[5,128]{1,0:T(8,128)S(1)} %copy-done.4, f32[5,128]{1,0:T(8,128)S(1)} %copy-done.5, bf16[5,256,128]{2,1,0:T(8,128)(2,1)S(1)} %bitcast.10, ...), custom_call_target="tpu_custom_call" | custom-call | tf_op jit(solution)/shard_map/norm_spatial/pallas_call | solution.py:290
  38.7 2.8 %collective-permute-start.2 = (bf16[2,3,256,128]{3,2,1,0:T(8,128)(2,1)S(1)}, bf16[2,3,256,128]{3,2,1,0:T(8,128)(2,1)S(1)}, u32[]{:S(2)}, u32[]{:S(2)}) collective-permute-start(bf16[2,3,256,128]{3,2,1,0:T(8,128)(2,1)S(1)} %get-tuple-element.18.refs_3_), channel_id=1, source_target_pairs={{0,4},{4,0},{8,12},{12,8},{16,20},{20,16},{24,28},{28,24},{32,36},... | collective-permute-start | bytes 1179656 | tf_op jit(solution)/shard_map/ppermute | solution.py:203
  41.5 1.3 %collective-permute-start.1 = (bf16[2,3,256,128]{3,2,1,0:T(8,128)(2,1)S(1)}, bf16[2,3,256,128]{3,2,1,0:T(8,128)(2,1)S(1)}, u32[]{:S(2)}, u32[]{:S(2)}) collective-permute-start(bf16[2,3,256,128]{3,2,1,0:T(8,128)(2,1)S(1)} %get-tuple-element.18.refs_3_), channel_id=1, source_target_pairs={{8,0},{12,4},{16,8},{20,12},{24,16},{28,20},{32,24},{36,28},{40,32... | collective-permute-start | bytes 1179656 | tf_op jit(solution)/shard_map/ppermute | solution.py:203
  42.8 4.0 %collective-permute-start = (bf16[2,3,256,128]{3,2,1,0:T(8,128)(2,1)S(1)}, bf16[2,3,256,128]{3,2,1,0:T(8,128)(2,1)S(1)}, u32[]{:S(2)}, u32[]{:S(2)}) collective-permute-start(bf16[2,3,256,128]{3,2,1,0:T(8,128)(2,1)S(1)} %get-tuple-element.18.refs_3_), channel_id=1, source_target_pairs={{0,8},{4,12},{8,16},{12,20},{16,24},{20,28},{24,32},{28,36},{32,40... | collective-permute-start | bytes 1179656 | tf_op jit(solution)/shard_map/ppermute | solution.py:203
  47.0 0.6 copy-done.7
  47.6 0.6 multiply_reduce_fusion
  48.2 0.1 broadcast_in_dim.29
  48.2 0.1 reshape_reshape.3.bias_ref
  48.3 16.5 %all-to-all-done.x_ref = bf16[128,6,2,128]{3,2,1,0:T(2,128)(2,1)S(1)} async-done(((bf16[128,6,2,128]{3,2,1,0:T(2,128)(2,1)}), bf16[128,6,2,128]{3,2,1,0:T(2,128)(2,1)S(1)}, u32[]{:S(2)}, u32[]{:S(2)}) %all-to-all-start) | async-done | bytes 393248 | tf_op jit(solution)/shard_map/all_to_all | solution.py:250
  64.8 1.4 %temporal.1 = bf16[128,2,2,128]{3,2,1,0:T(2,128)(2,1)} custom-call(bf16[128,6,2,128]{3,2,1,0:T(2,128)(2,1)S(1)} %all-to-all-done.x_ref), custom_call_target="tpu_custom_call" | custom-call | tf_op jit(solution)/shard_map/temporal/pallas_call | solution.py:300
  66.2 13.1 %all-to-all-start.1 = ((bf16[128,2,2,128]{3,2,1,0:T(2,128)(2,1)}), bf16[128,2,2,128]{3,2,1,0:T(2,128)(2,1)S(1)}, u32[]{:S(2)}, u32[]{:S(2)}) async-start(bf16[128,2,2,128]{3,2,1,0:T(2,128)(2,1)} %temporal.1), calls=%async_computation.1 | async-start | bytes 262144 | tf_op jit(solution)/shard_map/all_to_all | solution.py:250
  79.4 3.5 %collective-permute-start.3 = (bf16[2,3,256,128]{3,2,1,0:T(8,128)(2,1)S(1)}, bf16[2,3,256,128]{3,2,1,0:T(8,128)(2,1)S(1)}, u32[]{:S(2)}, u32[]{:S(2)}) collective-permute-start(bf16[2,3,256,128]{3,2,1,0:T(8,128)(2,1)S(1)} %broadcast_select_fusion), channel_id=1, source_target_pairs={{4,8},{8,4},{12,16},{16,12},{20,24},{24,20},{28,32},{32,28},{36,40... | collective-permute-start | bytes 1179656 | tf_op jit(solution)/shard_map/ppermute | solution.py:203
  82.9 1.9 %collective-permute-start.4 = (bf16[2,3,256,128]{3,2,1,0:T(8,128)(2,1)S(1)}, bf16[2,3,256,128]{3,2,1,0:T(8,128)(2,1)S(1)}, u32[]{:S(2)}, u32[]{:S(2)}) collective-permute-start(bf16[2,3,256,128]{3,2,1,0:T(8,128)(2,1)S(1)} %collective-permute-done.refs_1_), channel_id=1, source_target_pairs={{0,4},{4,0},{8,12},{12,8},{16,20},{20,16},{24,28},{28,24},{32,36},... | collective-permute-start | bytes 1179656 | tf_op jit(solution)/shard_map/ppermute | solution.py:203
  84.8 2.4 %collective-permute-start.5 = (bf16[2,3,256,128]{3,2,1,0:T(8,128)(2,1)S(1)}, bf16[2,3,256,128]{3,2,1,0:T(8,128)(2,1)S(1)}, u32[]{:S(2)}, u32[]{:S(2)}) collective-permute-start(bf16[2,3,256,128]{3,2,1,0:T(8,128)(2,1)S(1)} %collective-permute-done.1.refs_5_), channel_id=1, source_target_pairs={{0,4},{4,0},{8,12},{12,8},{16,20},{20,16},{24,28},{28,24},{32,36},... | collective-permute-start | bytes 1179656 | tf_op jit(solution)/shard_map/ppermute | solution.py:203
  87.3 0.2 convert_reduce_fusion
  87.4 0.1 select_reduce_fusion.order_ref
  87.5 3.6 %collective-permute-done.3.refs_0_ = bf16[2,3,256,128]{3,2,1,0:T(8,128)(2,1)S(1)} collective-permute-done((bf16[2,3,256,128]{3,2,1,0:T(8,128)(2,1)S(1)}, bf16[2,3,256,128]{3,2,1,0:T(8,128)(2,1)S(1)}, u32[]{:S(2)}, u32[]{:S(2)}) %collective-permute-start.3) | collective-permute-done | bytes 393248 | tf_op jit(solution)/shard_map/ppermute | solution.py:203
  91.2 3.7 %spatial.1.spatial_ref = bf16[5,256,128]{2,1,0:T(8,128)(2,1)} custom-call(s32[5]{0:T(128)S(1)} %select_reduce_fusion.order_ref, f32[4,1792]{1,0:T(4,128)S(1)} %reshape_reshape.3.bias_ref, bf16[3,256,128]{2,1,0:T(8,128)(2,1)S(1)} %get-tuple-element.20.q_ref, bf16[2,3,256,128]{3,2,1,0:T(8,128)(2,1)S(1)} %collective-permute-done.3.refs_0_, ...), custom_call_target="tpu_custom_call" | custom-call | tf_op jit(solution)/shard_map/spatial/pallas_call | solution.py:319
  94.9 1.8 %all-to-all-done.1.moved_ref = bf16[128,2,2,128]{3,2,1,0:T(2,128)(2,1)S(1)} async-done(((bf16[128,2,2,128]{3,2,1,0:T(2,128)(2,1)}), bf16[128,2,2,128]{3,2,1,0:T(2,128)(2,1)S(1)}, u32[]{:S(2)}, u32[]{:S(2)}) %all-to-all-start.1) | async-done | bytes 131104 | tf_op jit(solution)/shard_map/all_to_all | solution.py:250
  96.7 1.3 %join.1 = bf16[5,256,128]{2,1,0:T(8,128)(2,1)} custom-call(s32[5]{0:T(128)S(1)} %select_reduce_fusion.order_ref, bf16[128,2,2,128]{3,2,1,0:T(2,128)(2,1)S(1)} %all-to-all-done.1.moved_ref, bf16[5,256,128]{2,1,0:T(8,128)(2,1)} %spatial.1.spatial_ref), custom_call_target="tpu_custom_call", output_to_operand_aliasing={{}: (2, {})} | custom-call | tf_op jit(solution)/shard_map/join/pallas_call | solution.py:332
  (32 shorter events, 0.2 us)
Async XLA Ops:
  12.2 24.7 %copy-start.2 = (bf16[256,5,128]{2,0,1:T(8,128)(2,1)S(1)}, bf16[256,5,128]{2,0,1:T(8,128)(2,1)}, u32[]{:S(2)}) copy-start(bf16[256,5,128]{2,0,1:T(8,128)(2,1)} %param.12) | copy-start | bytes 983044
  15.1 21.8 %copy-start = (bf16[256,5,128]{2,0,1:T(8,128)(2,1)S(1)}, bf16[256,5,128]{2,0,1:T(8,128)(2,1)}, u32[]{:S(2)}) copy-start(bf16[256,5,128]{2,0,1:T(8,128)(2,1)} %param.10) | copy-start | bytes 983044
  15.1 21.8 %copy-start.1 = (bf16[256,5,128]{2,0,1:T(8,128)(2,1)S(1)}, bf16[256,5,128]{2,0,1:T(8,128)(2,1)}, u32[]{:S(2)}) copy-start(bf16[256,5,128]{2,0,1:T(8,128)(2,1)} %param.11) | copy-start | bytes 983044
  15.1 21.8 %copy-start.3 = (f32[2,256]{1,0:T(2,128)S(1)}, f32[2,256]{1,0:T(2,128)}, u32[]{:S(2)}) copy-start(f32[2,256]{1,0:T(2,128)} %psum.7.sums_hbm.sums_ref) | copy-start | bytes 6148
  15.2 21.8 %copy-start.4 = (f32[5,128]{1,0:T(8,128)S(1)}, f32[5,128]{1,0:T(8,128)}, u32[]{:S(2)}) copy-start(f32[5,128]{1,0:T(8,128)} %q_gain_ref.1) | copy-start | bytes 7684
  15.2 21.8 %copy-start.5 = (f32[5,128]{1,0:T(8,128)S(1)}, f32[5,128]{1,0:T(8,128)}, u32[]{:S(2)}) copy-start(f32[5,128]{1,0:T(8,128)} %k_gain_ref.1) | copy-start | bytes 7684
  15.2 21.8 %copy-start.6 = (s32[5]{0:T(128)S(1)}, s32[5]{0:T(128)}, u32[]{:S(2)}) copy-start(s32[5]{0:T(128)} %class_ref.3) | copy-start | bytes 64
  15.2 49.6 %all-to-all-start = ((bf16[128,6,2,128]{3,2,1,0:T(2,128)(2,1)}), bf16[128,6,2,128]{3,2,1,0:T(2,128)(2,1)S(1)}, u32[]{:S(2)}, u32[]{:S(2)}) async-start(bf16[128,6,2,128]{3,2,1,0:T(2,128)(2,1)} %norm_temporal.1), calls=%async_computation | async-start | bytes 786432 | tf_op jit(solution)/shard_map/all_to_all | solution.py:250
  37.0 9.9 %copy-start.9 = (s32[7]{0:T(128)S(1)}, s32[7]{0:T(128)}, u32[]{:S(2)}) copy-start(s32[7]{0:T(128)} %constant.36.clone) | copy-start | bytes 88
  37.0 9.9 %copy-start.10 = (s32[7]{0:T(128)S(1)}, s32[7]{0:T(128)}, u32[]{:S(2)}) copy-start(s32[7]{0:T(128)} %constant.35.clone) | copy-start | bytes 88
  37.0 9.9 %copy-start.8 = (s32[1,7]{1,0:T(1,128)S(1)}, s32[1,7]{1,0:T(1,128)}, u32[]{:S(2)}) copy-start(s32[1,7]{1,0:T(1,128)} %param.16) | copy-start | bytes 88
  38.7 27.5 %collective-permute-start.2 = (bf16[2,3,256,128]{3,2,1,0:T(8,128)(2,1)S(1)}, bf16[2,3,256,128]{3,2,1,0:T(8,128)(2,1)S(1)}, u32[]{:S(2)}, u32[]{:S(2)}) collective-permute-start(bf16[2,3,256,128]{3,2,1,0:T(8,128)(2,1)S(1)} %get-tuple-element.18.refs_3_), channel_id=1, source_target_pairs={{0,4},{4,0},{8,12},{12,8},{16,20},{20,16},{24,28},{28,24},{32,36},... | collective-permute-start | bytes 1179656 | tf_op jit(solution)/shard_map/ppermute | solution.py:203
  41.5 24.7 %collective-permute-start.1 = (bf16[2,3,256,128]{3,2,1,0:T(8,128)(2,1)S(1)}, bf16[2,3,256,128]{3,2,1,0:T(8,128)(2,1)S(1)}, u32[]{:S(2)}, u32[]{:S(2)}) collective-permute-start(bf16[2,3,256,128]{3,2,1,0:T(8,128)(2,1)S(1)} %get-tuple-element.18.refs_3_), channel_id=1, source_target_pairs={{8,0},{12,4},{16,8},{20,12},{24,16},{28,20},{32,24},{36,28},{40,32... | collective-permute-start | bytes 1179656 | tf_op jit(solution)/shard_map/ppermute | solution.py:203
  42.8 23.4 %collective-permute-start = (bf16[2,3,256,128]{3,2,1,0:T(8,128)(2,1)S(1)}, bf16[2,3,256,128]{3,2,1,0:T(8,128)(2,1)S(1)}, u32[]{:S(2)}, u32[]{:S(2)}) collective-permute-start(bf16[2,3,256,128]{3,2,1,0:T(8,128)(2,1)S(1)} %get-tuple-element.18.refs_3_), channel_id=1, source_target_pairs={{0,8},{4,12},{8,16},{12,20},{16,24},{20,28},{24,32},{28,36},{32,40... | collective-permute-start | bytes 1179656 | tf_op jit(solution)/shard_map/ppermute | solution.py:203
  46.9 0.7 copy-start.7
  66.2 30.5 %all-to-all-start.1 = ((bf16[128,2,2,128]{3,2,1,0:T(2,128)(2,1)}), bf16[128,2,2,128]{3,2,1,0:T(2,128)(2,1)S(1)}, u32[]{:S(2)}, u32[]{:S(2)}) async-start(bf16[128,2,2,128]{3,2,1,0:T(2,128)(2,1)} %temporal.1), calls=%async_computation.1 | async-start | bytes 262144 | tf_op jit(solution)/shard_map/all_to_all | solution.py:250
  79.4 11.8 %collective-permute-start.3 = (bf16[2,3,256,128]{3,2,1,0:T(8,128)(2,1)S(1)}, bf16[2,3,256,128]{3,2,1,0:T(8,128)(2,1)S(1)}, u32[]{:S(2)}, u32[]{:S(2)}) collective-permute-start(bf16[2,3,256,128]{3,2,1,0:T(8,128)(2,1)S(1)} %broadcast_select_fusion), channel_id=1, source_target_pairs={{4,8},{8,4},{12,16},{16,12},{20,24},{24,20},{28,32},{32,28},{36,40... | collective-permute-start | bytes 1179656 | tf_op jit(solution)/shard_map/ppermute | solution.py:203
  82.9 8.3 %collective-permute-start.4 = (bf16[2,3,256,128]{3,2,1,0:T(8,128)(2,1)S(1)}, bf16[2,3,256,128]{3,2,1,0:T(8,128)(2,1)S(1)}, u32[]{:S(2)}, u32[]{:S(2)}) collective-permute-start(bf16[2,3,256,128]{3,2,1,0:T(8,128)(2,1)S(1)} %collective-permute-done.refs_1_), channel_id=1, source_target_pairs={{0,4},{4,0},{8,12},{12,8},{16,20},{20,16},{24,28},{28,24},{32,36},... | collective-permute-start | bytes 1179656 | tf_op jit(solution)/shard_map/ppermute | solution.py:203
  84.8 6.3 %collective-permute-start.5 = (bf16[2,3,256,128]{3,2,1,0:T(8,128)(2,1)S(1)}, bf16[2,3,256,128]{3,2,1,0:T(8,128)(2,1)S(1)}, u32[]{:S(2)}, u32[]{:S(2)}) collective-permute-start(bf16[2,3,256,128]{3,2,1,0:T(8,128)(2,1)S(1)} %collective-permute-done.1.refs_5_), channel_id=1, source_target_pairs={{0,4},{4,0},{8,12},{12,8},{16,20},{20,16},{24,28},{28,24},{32,36},... | collective-permute-start | bytes 1179656 | tf_op jit(solution)/shard_map/ppermute | solution.py:203

commit v5 on v3

--- a/solution.py
+++ b/solution.py
@@ -15,6 +15,7 @@
 NT = 4
 FRAMES = 128
 HEADS = 20
+N_HEAD = HEADS // GROUP
 LOG2E = 1.4426950408889634
 SCALE = SIZE ** (-0.5) * LOG2E
 UNSEEN = -1e30
@@ -59,7 +60,9 @@
                 fetches[(row * GROUP + head) * 2 + part].wait()
             part = x_buf[head].astype(F32)
             total = total + part * part
-        sums_ref[row : row + 1] = jnp.sum(total.T, axis=0, keepdims=True)
+        sums = jnp.sum(total.T, axis=0, keepdims=True)
+        for member in range(N_HEAD):
+            sums_ref[member, row : row + 1] = sums
 
 
 def fetched(refs, heads, buf_ref, sems):
@@ -73,7 +76,7 @@
 
 
 def factors_of(sums_ref):
-    factors = lax.rsqrt(sums_ref[...] / (HEADS * SIZE) + 1e-06)
+    factors = lax.rsqrt(jnp.sum(sums_ref[...], axis=0) / (HEADS * SIZE) + 1e-06)
     return [jnp.broadcast_to(factors[row : row + 1], (SIZE, POS)).T for row in range(2)]
 
 
@@ -230,7 +233,7 @@
     q, k, v = (jnp.transpose(a, (1, 0, 2)) for a in (query, key, value))
     sums = pl.pallas_call(
         sums_kernel,
-        out_shape=jax.ShapeDtypeStruct((2, POS), F32),
+        out_shape=jax.ShapeDtypeStruct((N_HEAD, 2, POS), F32),
         in_specs=[whole(pl.ANY)] * 2,
         out_specs=whole(),
         scratch_shapes=[
@@ -241,7 +244,7 @@
         compiler_params=params(60),
         name="sums",
     )(q, k)
-    sums = lax.psum(sums, "head")
+    sums = lax.all_to_all(sums, "head", split_axis=0, concat_axis=0, tiled=True)
     norm_specs = [whole(pltpu.SMEM)] + [whole()] * 3 + [whole(pl.ANY)] * 3
     chunk = pl.pallas_call(
         norm_temporal_kernel,

time: 98.5 us -> 97 us (0.985)
  blocking collectives: 10.3 us -> 9.3 us
    psum x1 -> x0, blocking collectives: 10.3 us -> none  [shards(): sums = lax.psum(sums, 'head')]
    all_to_all x0 -> x1, blocking collectives: none -> 9.3 us  [shards(): sums = lax.all_to_all(sums, 'head', split_axis=0, concat_axis=0, tiled=True)]
where the time goes in v5:
time: 97 us; the launch traced here: 96.3 us
  starting transfers between devices  50.2 us (52%)
  waiting for transfers between devices  21.3 us (22%)
  Pallas kernels  12.8 us (13%)
  blocking collectives  9.3 us (10%)
  local copies, waits for them, and re-layouts  1.48 us (2%)
  other arithmetic  0.98 us (1%)
    all_to_all x2, starting transfers between devices, swap_all(): return lax.all_to_all(block, 'ctx', split_axis=0, concat_axis=0, tiled=True)  34.3 us
    all_to_all x2, waiting for transfers between devices, swap_all(): return lax.all_to_all(block, 'ctx', split_axis=0, concat_axis=0, tiled=True)  17.6 us
    ppermute x6, starting transfers between devices, route(): return lax.ppermute(block, 'ctx', pairs)  16 us
    all_to_all x1, blocking collectives, shards(): sums = lax.all_to_all(sums, 'head', split_axis=0, concat_axis=0, tiled=True)  9.3 us
    pallas_call x1, Pallas kernels, shards(): pl.pallas_call(spatial_kernel, out_shape=bf16(GROUP, POS, SIZE), in_specs...  3.71 us
    ppermute x6, waiting for transfers between devices, route(): return lax.ppermute(block, 'ctx', pairs)  3.64 us
    pallas_call x1, Pallas kernels, shards(): pl.pallas_call(norm_temporal_kernel, out_shape=bf16(FRAMES, 3 * TEMP, SUB...  2.76 us
    pallas_call x1, Pallas kernels, shards(): pl.pallas_call(sums_kernel, out_shape=jax.ShapeDtypeStruct((N_HEAD, 2, PO...  1.96 us
  transfers between devices with their start and end apart: 8, of which 3 were waited for; matrix products, arithmetic and copies ran while one was open for 1% of the time, Pallas kernels for 7%

profile of v5, /device:TPU:1, one launch (start us, length us, event | category | flops | bytes accessed | tf_op | source)
XLA Modules:
  0.0 96.3 jit_solution(1941370609559894662)
XLA Ops:
  0.0 2.0 %sums.1 = f32[4,2,256]{2,1,0:T(2,128)} custom-call(bf16[5,256,128]{2,1,0:T(8,128)(2,1)} %bitcast.8, bf16[5,256,128]{2,1,0:T(8,128)(2,1)} %bitcast.11), custom_call_target="tpu_custom_call" | custom-call | tf_op jit(solution)/shard_map/sums/pallas_call | solution.py:234
  2.0 9.3 %all_to_all.15.sums_ref = f32[4,2,256]{2,1,0:T(2,128)} all-to-all(f32[4,2,256]{2,1,0:T(2,128)} %sums.1), channel_id=1, replica_groups=mesh['ctx'=128,'head'=4] {'head'}, dimensions={0} | all-to-all | bytes 16384 | tf_op jit(solution)/shard_map/all_to_all | solution.py:247
  11.3 2.8 %norm_temporal.1 = bf16[128,6,2,128]{3,2,1,0:T(2,128)(2,1)} custom-call(s32[5]{0:T(128)} %class_ref.3, f32[4,2,256]{2,1,0:T(2,128)} %all_to_all.15.sums_ref, f32[5,128]{1,0:T(8,128)} %q_gain_ref.3, f32[5,128]{1,0:T(8,128)} %k_gain_ref.3, bf16[5,256,128]{2,1,0:T(8,128)(2,1)} %bitcast.9, bf16[5,256,128]{2,1,0:T(8,128)(2,1)} %bitcast.12, ...), custom_call_target="tpu_custom_call" | custom-call | tf_op jit(solution)/shard_map/norm_temporal/pallas_call | solution.py:249
  14.1 21.1 %all-to-all-start.1 = ((bf16[128,6,2,128]{3,2,1,0:T(2,128)(2,1)}), bf16[128,6,2,128]{3,2,1,0:T(2,128)(2,1)S(1)}, u32[]{:S(2)}, u32[]{:S(2)}) async-start(bf16[128,6,2,128]{3,2,1,0:T(2,128)(2,1)} %norm_temporal.1), calls=%async_computation.1 | async-start | bytes 786432 | tf_op jit(solution)/shard_map/all_to_all | solution.py:229
  35.3 0.6 copy-done.9
  36.0 0.6 copy-done.6
  36.6 1.7 %norm_spatial.1 = (bf16[3,256,128]{2,1,0:T(8,128)(2,1)S(1)}, bf16[2,3,256,128]{3,2,1,0:T(8,128)(2,1)S(1)}) custom-call(s32[5]{0:T(128)S(1)} %copy-done.6, f32[4,2,256]{2,1,0:T(2,128)S(1)} %copy-done.3, f32[5,128]{1,0:T(8,128)S(1)} %copy-done.4, f32[5,128]{1,0:T(8,128)S(1)} %copy-done.5, bf16[5,256,128]{2,1,0:T(8,128)(2,1)S(1)} %bitcast.10, ...), custom_call_target="tpu_custom_call" | custom-call | tf_op jit(solution)/shard_map/norm_spatial/pallas_call | solution.py:260
  38.3 2.8 %collective-permute-start.2 = (bf16[2,3,256,128]{3,2,1,0:T(8,128)(2,1)S(1)}, bf16[2,3,256,128]{3,2,1,0:T(8,128)(2,1)S(1)}, u32[]{:S(2)}, u32[]{:S(2)}) collective-permute-start(bf16[2,3,256,128]{3,2,1,0:T(8,128)(2,1)S(1)} %get-tuple-element.18.refs_3_), channel_id=1, source_target_pairs={{0,4},{4,0},{8,12},{12,8},{16,20},{20,16},{24,28},{28,24},{32,36},... | collective-permute-start | bytes 1179656 | tf_op jit(solution)/shard_map/ppermute | solution.py:182
  41.1 1.3 %collective-permute-start.1 = (bf16[2,3,256,128]{3,2,1,0:T(8,128)(2,1)S(1)}, bf16[2,3,256,128]{3,2,1,0:T(8,128)(2,1)S(1)}, u32[]{:S(2)}, u32[]{:S(2)}) collective-permute-start(bf16[2,3,256,128]{3,2,1,0:T(8,128)(2,1)S(1)} %get-tuple-element.18.refs_3_), channel_id=1, source_target_pairs={{8,0},{12,4},{16,8},{20,12},{24,16},{28,20},{32,24},{36,28},{40,32... | collective-permute-start | bytes 1179656 | tf_op jit(solution)/shard_map/ppermute | solution.py:182
  42.4 4.0 %collective-permute-start = (bf16[2,3,256,128]{3,2,1,0:T(8,128)(2,1)S(1)}, bf16[2,3,256,128]{3,2,1,0:T(8,128)(2,1)S(1)}, u32[]{:S(2)}, u32[]{:S(2)}) collective-permute-start(bf16[2,3,256,128]{3,2,1,0:T(8,128)(2,1)S(1)} %get-tuple-element.18.refs_3_), channel_id=1, source_target_pairs={{0,8},{4,12},{8,16},{12,20},{16,24},{20,28},{24,32},{28,36},{32,40... | collective-permute-start | bytes 1179656 | tf_op jit(solution)/shard_map/ppermute | solution.py:182
  46.5 0.6 multiply_reduce_fusion
  47.2 0.1 reshape_reshape.3.bias_ref
  47.3 15.8 %all-to-all-done.1.x_ref = bf16[128,6,2,128]{3,2,1,0:T(2,128)(2,1)S(1)} async-done(((bf16[128,6,2,128]{3,2,1,0:T(2,128)(2,1)}), bf16[128,6,2,128]{3,2,1,0:T(2,128)(2,1)S(1)}, u32[]{:S(2)}, u32[]{:S(2)}) %all-to-all-start.1) | async-done | bytes 393248 | tf_op jit(solution)/shard_map/all_to_all | solution.py:229
  63.1 1.4 %temporal.1 = bf16[128,2,2,128]{3,2,1,0:T(2,128)(2,1)} custom-call(bf16[128,6,2,128]{3,2,1,0:T(2,128)(2,1)S(1)} %all-to-all-done.1.x_ref), custom_call_target="tpu_custom_call" | custom-call | tf_op jit(solution)/shard_map/temporal/pallas_call | solution.py:270
  64.5 13.1 %all-to-all-start.2 = ((bf16[128,2,2,128]{3,2,1,0:T(2,128)(2,1)}), bf16[128,2,2,128]{3,2,1,0:T(2,128)(2,1)S(1)}, u32[]{:S(2)}, u32[]{:S(2)}) async-start(bf16[128,2,2,128]{3,2,1,0:T(2,128)(2,1)} %temporal.1), calls=%async_computation.2 | async-start | bytes 262144 | tf_op jit(solution)/shard_map/all_to_all | solution.py:229
  77.7 3.5 %collective-permute-start.3 = (bf16[2,3,256,128]{3,2,1,0:T(8,128)(2,1)S(1)}, bf16[2,3,256,128]{3,2,1,0:T(8,128)(2,1)S(1)}, u32[]{:S(2)}, u32[]{:S(2)}) collective-permute-start(bf16[2,3,256,128]{3,2,1,0:T(8,128)(2,1)S(1)} %broadcast_select_fusion), channel_id=1, source_target_pairs={{4,8},{8,4},{12,16},{16,12},{20,24},{24,20},{28,32},{32,28},{36,40... | collective-permute-start | bytes 1179656 | tf_op jit(solution)/shard_map/ppermute | solution.py:182
  81.2 1.9 %collective-permute-start.4 = (bf16[2,3,256,128]{3,2,1,0:T(8,128)(2,1)S(1)}, bf16[2,3,256,128]{3,2,1,0:T(8,128)(2,1)S(1)}, u32[]{:S(2)}, u32[]{:S(2)}) collective-permute-start(bf16[2,3,256,128]{3,2,1,0:T(8,128)(2,1)S(1)} %collective-permute-done.refs_1_), channel_id=1, source_target_pairs={{0,4},{4,0},{8,12},{12,8},{16,20},{20,16},{24,28},{28,24},{32,36},... | collective-permute-start | bytes 1179656 | tf_op jit(solution)/shard_map/ppermute | solution.py:182
  83.1 2.4 %collective-permute-start.5 = (bf16[2,3,256,128]{3,2,1,0:T(8,128)(2,1)S(1)}, bf16[2,3,256,128]{3,2,1,0:T(8,128)(2,1)S(1)}, u32[]{:S(2)}, u32[]{:S(2)}) collective-permute-start(bf16[2,3,256,128]{3,2,1,0:T(8,128)(2,1)S(1)} %collective-permute-done.1.refs_5_), channel_id=1, source_target_pairs={{0,4},{4,0},{8,12},{12,8},{16,20},{20,16},{24,28},{28,24},{32,36},... | collective-permute-start | bytes 1179656 | tf_op jit(solution)/shard_map/ppermute | solution.py:182
  85.6 0.2 convert_reduce_fusion
  85.7 0.1 select_reduce_fusion.order_ref
  85.8 3.6 %collective-permute-done.3.refs_0_ = bf16[2,3,256,128]{3,2,1,0:T(8,128)(2,1)S(1)} collective-permute-done((bf16[2,3,256,128]{3,2,1,0:T(8,128)(2,1)S(1)}, bf16[2,3,256,128]{3,2,1,0:T(8,128)(2,1)S(1)}, u32[]{:S(2)}, u32[]{:S(2)}) %collective-permute-start.3) | collective-permute-done | bytes 393248 | tf_op jit(solution)/shard_map/ppermute | solution.py:182
  89.5 3.7 %spatial.1.spatial_ref = bf16[5,256,128]{2,1,0:T(8,128)(2,1)} custom-call(s32[5]{0:T(128)S(1)} %select_reduce_fusion.order_ref, f32[4,1792]{1,0:T(4,128)S(1)} %reshape_reshape.3.bias_ref, bf16[3,256,128]{2,1,0:T(8,128)(2,1)S(1)} %get-tuple-element.20.q_ref, bf16[2,3,256,128]{3,2,1,0:T(8,128)(2,1)S(1)} %collective-permute-done.3.refs_0_, ...), custom_call_target="tpu_custom_call" | custom-call | tf_op jit(solution)/shard_map/spatial/pallas_call | solution.py:285
  93.2 1.8 %all-to-all-done.2.moved_ref = bf16[128,2,2,128]{3,2,1,0:T(2,128)(2,1)S(1)} async-done(((bf16[128,2,2,128]{3,2,1,0:T(2,128)(2,1)}), bf16[128,2,2,128]{3,2,1,0:T(2,128)(2,1)S(1)}, u32[]{:S(2)}, u32[]{:S(2)}) %all-to-all-start.2) | async-done | bytes 131104 | tf_op jit(solution)/shard_map/all_to_all | solution.py:229
  95.0 1.3 %join.1 = bf16[5,256,128]{2,1,0:T(8,128)(2,1)} custom-call(s32[5]{0:T(128)S(1)} %select_reduce_fusion.order_ref, bf16[128,2,2,128]{3,2,1,0:T(2,128)(2,1)S(1)} %all-to-all-done.2.moved_ref, bf16[5,256,128]{2,1,0:T(8,128)(2,1)} %spatial.1.spatial_ref), custom_call_target="tpu_custom_call", output_to_operand_aliasing={{}: (2, {})} | custom-call | tf_op jit(solution)/shard_map/join/pallas_call | solution.py:298
  (32 shorter events, 0.3 us)
Async XLA Ops:
  11.3 24.7 %copy-start.2 = (bf16[256,5,128]{2,0,1:T(8,128)(2,1)S(1)}, bf16[256,5,128]{2,0,1:T(8,128)(2,1)}, u32[]{:S(2)}) copy-start(bf16[256,5,128]{2,0,1:T(8,128)(2,1)} %param.12) | copy-start | bytes 983044
  14.0 21.9 %copy-start = (bf16[256,5,128]{2,0,1:T(8,128)(2,1)S(1)}, bf16[256,5,128]{2,0,1:T(8,128)(2,1)}, u32[]{:S(2)}) copy-start(bf16[256,5,128]{2,0,1:T(8,128)(2,1)} %param.10) | copy-start | bytes 983044
  14.0 21.9 %copy-start.1 = (bf16[256,5,128]{2,0,1:T(8,128)(2,1)S(1)}, bf16[256,5,128]{2,0,1:T(8,128)(2,1)}, u32[]{:S(2)}) copy-start(bf16[256,5,128]{2,0,1:T(8,128)(2,1)} %param.11) | copy-start | bytes 983044
  14.1 21.9 %copy-start.5 = (f32[5,128]{1,0:T(8,128)S(1)}, f32[5,128]{1,0:T(8,128)}, u32[]{:S(2)}) copy-start(f32[5,128]{1,0:T(8,128)} %k_gain_ref.3) | copy-start | bytes 7684
  14.1 49.0 %all-to-all-start.1 = ((bf16[128,6,2,128]{3,2,1,0:T(2,128)(2,1)}), bf16[128,6,2,128]{3,2,1,0:T(2,128)(2,1)S(1)}, u32[]{:S(2)}, u32[]{:S(2)}) async-start(bf16[128,6,2,128]{3,2,1,0:T(2,128)(2,1)} %norm_temporal.1), calls=%async_computation.1 | async-start | bytes 786432 | tf_op jit(solution)/shard_map/all_to_all | solution.py:229
  35.2 0.7 copy-start.3
  35.2 0.7 copy-start.4
  35.2 0.7 copy-start.9
  35.3 0.7 copy-start.10
  35.9 0.7 copy-start.6
  36.6 9.8 %copy-start.8 = (s32[1,7]{1,0:T(1,128)S(1)}, s32[1,7]{1,0:T(1,128)}, u32[]{:S(2)}) copy-start(s32[1,7]{1,0:T(1,128)} %param.16) | copy-start | bytes 88
  38.3 8.2 %copy-start.7 = (s32[1,7,4,4]{1,3,2,0:T(4,128)S(1)}, s32[1,7,4,4]{1,3,2,0:T(4,128)}, u32[]{:S(2)}) copy-start(s32[1,7,4,4]{1,3,2,0:T(4,128)} %param.17) | copy-start | bytes 1348
  38.3 26.2 %collective-permute-start.2 = (bf16[2,3,256,128]{3,2,1,0:T(8,128)(2,1)S(1)}, bf16[2,3,256,128]{3,2,1,0:T(8,128)(2,1)S(1)}, u32[]{:S(2)}, u32[]{:S(2)}) collective-permute-start(bf16[2,3,256,128]{3,2,1,0:T(8,128)(2,1)S(1)} %get-tuple-element.18.refs_3_), channel_id=1, source_target_pairs={{0,4},{4,0},{8,12},{12,8},{16,20},{20,16},{24,28},{28,24},{32,36},... | collective-permute-start | bytes 1179656 | tf_op jit(solution)/shard_map/ppermute | solution.py:182
  41.1 23.4 %collective-permute-start.1 = (bf16[2,3,256,128]{3,2,1,0:T(8,128)(2,1)S(1)}, bf16[2,3,256,128]{3,2,1,0:T(8,128)(2,1)S(1)}, u32[]{:S(2)}, u32[]{:S(2)}) collective-permute-start(bf16[2,3,256,128]{3,2,1,0:T(8,128)(2,1)S(1)} %get-tuple-element.18.refs_3_), channel_id=1, source_target_pairs={{8,0},{12,4},{16,8},{20,12},{24,16},{28,20},{32,24},{36,28},{40,32... | collective-permute-start | bytes 1179656 | tf_op jit(solution)/shard_map/ppermute | solution.py:182
  42.4 22.1 %collective-permute-start = (bf16[2,3,256,128]{3,2,1,0:T(8,128)(2,1)S(1)}, bf16[2,3,256,128]{3,2,1,0:T(8,128)(2,1)S(1)}, u32[]{:S(2)}, u32[]{:S(2)}) collective-permute-start(bf16[2,3,256,128]{3,2,1,0:T(8,128)(2,1)S(1)} %get-tuple-element.18.refs_3_), channel_id=1, source_target_pairs={{0,8},{4,12},{8,16},{12,20},{16,24},{20,28},{24,32},{28,36},{32,40... | collective-permute-start | bytes 1179656 | tf_op jit(solution)/shard_map/ppermute | solution.py:182
  64.5 30.6 %all-to-all-start.2 = ((bf16[128,2,2,128]{3,2,1,0:T(2,128)(2,1)}), bf16[128,2,2,128]{3,2,1,0:T(2,128)(2,1)S(1)}, u32[]{:S(2)}, u32[]{:S(2)}) async-start(bf16[128,2,2,128]{3,2,1,0:T(2,128)(2,1)} %temporal.1), calls=%async_computation.2 | async-start | bytes 262144 | tf_op jit(solution)/shard_map/all_to_all | solution.py:229
  77.7 11.8 %collective-permute-start.3 = (bf16[2,3,256,128]{3,2,1,0:T(8,128)(2,1)S(1)}, bf16[2,3,256,128]{3,2,1,0:T(8,128)(2,1)S(1)}, u32[]{:S(2)}, u32[]{:S(2)}) collective-permute-start(bf16[2,3,256,128]{3,2,1,0:T(8,128)(2,1)S(1)} %broadcast_select_fusion), channel_id=1, source_target_pairs={{4,8},{8,4},{12,16},{16,12},{20,24},{24,20},{28,32},{32,28},{36,40... | collective-permute-start | bytes 1179656 | tf_op jit(solution)/shard_map/ppermute | solution.py:182
  81.2 8.3 %collective-permute-start.4 = (bf16[2,3,256,128]{3,2,1,0:T(8,128)(2,1)S(1)}, bf16[2,3,256,128]{3,2,1,0:T(8,128)(2,1)S(1)}, u32[]{:S(2)}, u32[]{:S(2)}) collective-permute-start(bf16[2,3,256,128]{3,2,1,0:T(8,128)(2,1)S(1)} %collective-permute-done.refs_1_), channel_id=1, source_target_pairs={{0,4},{4,0},{8,12},{12,8},{16,20},{20,16},{24,28},{28,24},{32,36},... | collective-permute-start | bytes 1179656 | tf_op jit(solution)/shard_map/ppermute | solution.py:182
  83.1 6.3 %collective-permute-start.5 = (bf16[2,3,256,128]{3,2,1,0:T(8,128)(2,1)S(1)}, bf16[2,3,256,128]{3,2,1,0:T(8,128)(2,1)S(1)}, u32[]{:S(2)}, u32[]{:S(2)}) collective-permute-start(bf16[2,3,256,128]{3,2,1,0:T(8,128)(2,1)S(1)} %collective-permute-done.1.refs_5_), channel_id=1, source_target_pairs={{0,4},{4,0},{8,12},{12,8},{16,20},{20,16},{24,28},{28,24},{32,36},... | collective-permute-start | bytes 1179656 | tf_op jit(solution)/shard_map/ppermute | solution.py:182
